TPU v7x, 256 devices: a whole 4x4x8 slice. The times are simulated.
256 devices in a mesh: section: 4 (over z_lo, core), ctx: 16 (over x, y), tp: 4 (over z_hi).
Axes of the slice: x: 4, y: 4, z: 8 (z_hi: 4, z_lo: 2; z = z_hi * 2 + z_lo), core: 2. Of those that a mesh axis runs over, the one named last changes fastest.
Arguments:
- layer_inputs: bfloat16 [4, 16384, 5120], P('section', 'ctx', 'tp'), may hold values from -6 to 6
- norm_gain: bfloat16 [4, 5120], P('section', 'tp'), may hold values from 0.25 to 1.75
- kv_weight: bfloat16 [4, 5120, 2048], P('section', None, 'tp'), may hold values from -0.078125 to 0.078125
- span_pages: int32 [4], replicated, may hold values from 1 to 512, 1024 in all
- page_owner: int32 [1024, 1], replicated, may hold values from 0 to 15; in each aligned block of 64 rows (0 to 63, 64 to 127, ...) at most 8 rows name the same one
- cache_len: int32 [4], replicated, may hold values from 1 to 8192
- cache_kv: bfloat16 [4, 4, 8192, 2048], P('section', None, 'ctx', 'tp'), may hold values from -6 to 6
- queries: bfloat16 [4, 4, 4, 4096], P('section', None, None, 'tp'), may hold values from -150 to 150
- new_kv: bfloat16 [4, 4, 4, 2048], P('section', None, None, 'tp'), may hold values from -6 to 6
Outputs:
- page_store: bfloat16 [4, 2048, 16, 2048], P('section', 'ctx', None, 'tp')
- attention: bfloat16 [4, 4, 4, 4096], P('section', None, None, 'tp')
All inputs are finite; a program needn't handle non-finite values.
Results may differ from a plain program's by a relative error of at most 0.013.
Values may be sent and summed in bfloat16 or wider, within the bound.
No kernel may reach another device: no remote copies, remote signals or barrier semaphores. Data moves between devices by JAX's collectives and lax.ppermute only.
A program may use at most 128 MiB of HBM per device.

v0:
```python
import jax
import jax.numpy as jnp
from jax import lax
from jax.sharding import PartitionSpec as P

D = 5120
HEAD_DIM = 128
SESSIONS = 4
STEPS = 4
PAGE = 16


epsilon = 1e-05
floor_value = -1e30


def from_behind(array, axis, by):
    peers = lax.axis_size(axis)
    pairs = [(i, i + by) for i in range(peers) if 0 <= i + by < peers]
    return lax.ppermute(array, axis, pairs)


def joined(part, axis, combine):
    gathered = jax.tree.map(lambda a: lax.all_gather(a, axis), part)

    def take(source):
        return jax.tree.map(lambda a: lax.dynamic_index_in_dim(a, source, 0, False), gathered)

    return lax.fori_loop(
        1, lax.axis_size(axis), lambda source, state: combine(state, take(source)), take(0)
    )


def split_local(block, per_group):
    shaped = block.reshape(block.shape[:-1] + (2, per_group, HEAD_DIM))
    return (shaped[..., 0, :, :], shaped[..., 1, :, :])


def combine(first, second):
    top = jnp.maximum(first[0], second[0])
    first_factor = jnp.exp(first[0] - top)
    second_factor = jnp.exp(second[0] - top)
    total = first[1] * first_factor + second[1] * second_factor
    mixed = first[2] * first_factor[..., None] + second[2] * second_factor[..., None]
    return (top, total, mixed)


def per_device(
    layer_inputs, norm_gain, kv_weight, span_pages, page_owner, cache_len, cache_kv, queries, new_kv
):
    sections = lax.axis_size("section")
    n_ctx = lax.axis_size("ctx")
    section_index = lax.axis_index("section")
    ctx_index = lax.axis_index("ctx")
    own_part = layer_inputs[0]
    hidden = own_part
    for step in range(1, sections):
        arrived = from_behind(hidden, "section", 1)
        advanced = (arrived.astype(jnp.float32) + own_part.astype(jnp.float32)).astype(jnp.bfloat16)
        hidden = jnp.where(section_index == step, advanced, hidden)
    weight = kv_weight[0]
    kv_cols = weight.shape[1]
    row_count = hidden.shape[0]
    wide = hidden.astype(jnp.float32)
    sums = lax.psum(jnp.sum(wide * wide, axis=1, keepdims=True), "tp")
    normed = (wide * lax.rsqrt(sums / D + epsilon) * norm_gain[0].astype(jnp.float32)).astype(
        jnp.bfloat16
    )
    fresh = jnp.dot(
        lax.all_gather(normed, "tp", axis=1, tiled=True), weight, preferred_element_type=jnp.float32
    ).astype(jnp.bfloat16)
    pages_dev = row_count // PAGE
    capacity = max(2, 2 * pages_dev // n_ctx)
    owner = page_owner[:, 0]
    total_pages = owner.shape[0]
    page_index = jnp.arange(total_pages, dtype=jnp.int32)
    ends = jnp.cumsum(span_pages)
    page_session = jnp.sum((ends[None, :] <= page_index[:, None]).astype(jnp.int32), axis=1)
    onehot = (owner[:, None] == jnp.arange(n_ctx, dtype=jnp.int32)[None, :]).astype(jnp.int32)
    running = jnp.cumsum(onehot.reshape(n_ctx, pages_dev, n_ctx), axis=1).reshape(
        total_pages, n_ctx
    )
    rank_all = jnp.sum((running - 1) * onehot, axis=1)
    start_page = ctx_index * pages_dev
    mine_owner = lax.dynamic_slice_in_dim(owner, start_page, pages_dev)
    mine_rank = lax.dynamic_slice_in_dim(rank_all, start_page, pages_dev)
    target = mine_owner * capacity + mine_rank
    paged = fresh.reshape(pages_dev, PAGE, kv_cols)
    outgoing = jnp.zeros((n_ctx * capacity, PAGE, kv_cols), jnp.bfloat16).at[target].set(paged)
    outgoing = outgoing.reshape(n_ctx, capacity, PAGE, kv_cols)
    received = lax.all_to_all(outgoing, "ctx", split_axis=0, concat_axis=0, tiled=True)
    page_store = received.reshape(1, n_ctx * capacity, PAGE, kv_cols)
    source = page_index // pages_dev
    flat = jnp.where(owner == ctx_index, source * capacity + rank_all, n_ctx * capacity)
    slot_session = (
        jnp.full((n_ctx * capacity,), -1, jnp.int32).at[flat].set(page_session, mode="drop")
    )
    page_rows = received.reshape(n_ctx * capacity * PAGE, kv_cols)
    row_session = jnp.repeat(slot_session, PAGE, total_repeat_length=n_ctx * capacity * PAGE)
    per_group = kv_cols // (2 * HEAD_DIM)
    group = queries.shape[-1] // (HEAD_DIM * per_group)
    scale = HEAD_DIM ** (-0.5)
    heads = queries[0].reshape(SESSIONS, STEPS, per_group, group, HEAD_DIM)
    cache_keys, cache_values = split_local(cache_kv[0], per_group)
    page_keys, page_values = split_local(page_rows, per_group)
    local_len = cache_kv.shape[2]
    positions = ctx_index * local_len + jnp.arange(local_len, dtype=jnp.int32)
    cache_mask = (positions[None, :] < cache_len[:, None])[:, None, None, None, :]
    page_mask = (row_session[None, :] == jnp.arange(SESSIONS, dtype=jnp.int32)[:, None])[
        :, None, None, None, :
    ]
    cache_scores = (
        jnp.einsum("stkge,slke->stkgl", heads, cache_keys, preferred_element_type=jnp.float32)
        * scale
    )
    page_scores = (
        jnp.einsum("stkge,rke->stkgr", heads, page_keys, preferred_element_type=jnp.float32) * scale
    )
    peak = jnp.maximum(
        jnp.max(jnp.where(cache_mask, cache_scores, floor_value), axis=-1),
        jnp.max(jnp.where(page_mask, page_scores, floor_value), axis=-1),
    )
    cache_weights = jnp.where(cache_mask, jnp.exp(cache_scores - peak[..., None]), 0.0)
    page_weights = jnp.where(page_mask, jnp.exp(page_scores - peak[..., None]), 0.0)
    total = jnp.sum(cache_weights, axis=-1) + jnp.sum(page_weights, axis=-1)
    mixed = jnp.einsum(
        "stkgl,slke->stkge",
        cache_weights,
        cache_values.astype(jnp.float32),
        precision=lax.Precision.HIGHEST,
    )
    mixed = mixed + jnp.einsum(
        "stkgr,rke->stkge",
        page_weights,
        page_values.astype(jnp.float32),
        precision=lax.Precision.HIGHEST,
    )
    peak, total, mixed = joined((peak, total, mixed), "ctx", combine)
    new_keys, new_values = split_local(new_kv[0], per_group)
    new_scores = (
        jnp.einsum("stkge,suke->stkgu", heads, new_keys, preferred_element_type=jnp.float32) * scale
    )
    causal = (jnp.arange(STEPS)[None, :] <= jnp.arange(STEPS)[:, None])[None, :, None, None, :]
    new_peak = jnp.max(jnp.where(causal, new_scores, floor_value), axis=-1)
    top = jnp.maximum(peak, new_peak)
    old_factor = jnp.exp(peak - top)
    new_weights = jnp.where(causal, jnp.exp(new_scores - top[..., None]), 0.0)
    total = total * old_factor + jnp.sum(new_weights, axis=-1)
    mixed = mixed * old_factor[..., None] + jnp.einsum(
        "stkgu,suke->stkge",
        new_weights,
        new_values.astype(jnp.float32),
        precision=lax.Precision.HIGHEST,
    )
    attention = (
        (mixed / total[..., None])
        .reshape(1, SESSIONS, STEPS, group * per_group * HEAD_DIM)
        .astype(jnp.bfloat16)
    )
    return (page_store, attention)


def solution(mesh):
    return jax.shard_map(
        per_device,
        mesh=mesh,
        in_specs=(
            P("section", "ctx", "tp"),
            P("section", "tp"),
            P("section", None, "tp"),
            P(),
            P(),
            P(),
            P("section", None, "ctx", "tp"),
            P("section", None, None, "tp"),
            P("section", None, None, "tp"),
        ),
        out_specs=(P("section", "ctx", None, "tp"), P("section", None, None, "tp")),
        check_vma=False,
    )
```

profile of v0, /device:TPU:64, one launch (start us, length us, event | category | flops | bytes accessed | tf_op | source)
XLA Modules:
  0.0 461.2 jit_solution(8996543277510898014)
XLA Ops:
  7.2 3.3 collective-permute-start
  10.5 3.3 collective-permute-done
  13.8 4.8 %fusion.12 = bf16[1024,1280]{1,0:T(8,128)(2,1)} fusion(bf16[1024,1280]{1,0:T(8,128)(2,1)} %collective-permute-done, pred[]{:T(512)S(6)} %eq.56, bf16[1,1024,1280]{2,1,0:T(8,128)(2,1)} %param.13), kind=kLoop, calls=%fused_computation.27 | loop fusion | flops 6553600 | bytes 7864321 | tf_op jit(solution)/shard_map/jit(_where)/select_n | solution.py:60
  18.6 29.7 %collective-permute-start.1 = (bf16[1024,1280]{1,0:T(8,128)(2,1)}, bf16[1024,1280]{1,0:T(8,128)(2,1)}, u32[]{:S(2)}, u32[]{:S(2)}) collective-permute-start(bf16[1024,1280]{1,0:T(8,128)(2,1)} %fusion.12), channel_id=1, source_target_pairs={{0,64},{64,128},{128,192},{1,65},{65,129},{129,193},{2,66},{66,130... | collective-permute-start | bytes 7864328 | tf_op jit(solution)/shard_map/ppermute | solution.py:20
  48.3 3.3 collective-permute-done.1
  51.6 5.0 %fusion.14 = bf16[1024,1280]{1,0:T(8,128)(2,1)} fusion(bf16[1024,1280]{1,0:T(8,128)(2,1)} %fusion.12, bf16[1024,1280]{1,0:T(8,128)(2,1)} %collective-permute-done.1, pred[]{:T(512)S(6)} %eq.55, bf16[1,1024,1280]{2,1,0:T(8,128)(2,1)S(1)} %copy-done), kind=kLoop, calls=%fused_computation.29 | loop fusion | flops 6553600 | bytes 10485761 | tf_op jit(solution)/shard_map/jit(_where)/select_n | solution.py:60
  56.6 29.9 %collective-permute-start.2 = (bf16[1024,1280]{1,0:T(8,128)(2,1)}, bf16[1024,1280]{1,0:T(8,128)(2,1)}, u32[]{:S(2)}, u32[]{:S(2)}) collective-permute-start(bf16[1024,1280]{1,0:T(8,128)(2,1)} %fusion.14), channel_id=1, source_target_pairs={{0,64},{64,128},{128,192},{1,65},{65,129},{129,193},{2,66},{66,130... | collective-permute-start | bytes 7864328 | tf_op jit(solution)/shard_map/ppermute | solution.py:20
  86.6 3.3 collective-permute-done.2
  89.9 5.3 %fusion.4 = (f32[1024]{0:T(1024)S(1)}, bf16[1024,1280]{1,0:T(8,128)(2,1)}) fusion(bf16[1024,1280]{1,0:T(8,128)(2,1)} %fusion.14, bf16[1,1024,1280]{2,1,0:T(8,128)(2,1)S(1)} %copy-done, bf16[1024,1280]{1,0:T(8,128)(2,1)} %collective-permute-done.2, pred[]{:T(512)S(6)} %eq.54), kind=kLoop, calls=%fused_computation.19 | loop fusion | flops 10484736 | bytes 10489857 | tf_op jit(solution)/shard_map/reduce_sum | solution.py:65
  95.2 11.2 %psum.7 = f32[1024,1]{0,1:T(1,128)S(1)} all-reduce(f32[1024,1]{0,1:T(1,128)S(1)} %bitcast.146), channel_id=1, replica_groups=mesh['section'=4,'ctx'=16,'tp'=4] {'tp'}, use_global_device_ids=true, to_apply=%region_3.4 | all-reduce | flops 1024 | bytes 8192 | tf_op jit(solution)/shard_map/psum | solution.py:65
  106.4 3.9 fusion.6
  110.3 0.5 broadcast.246
  110.8 0.1 copy-done.5
  111.0 0.7 reduce.8
  111.7 0.1 copy.101
  111.8 1.4 select_reduce_fusion.1
  113.4 0.1 reduce_sum.61
  113.5 0.2 reduce-window.12
  113.7 0.1 compare_select_fusion.4
  113.8 210.3 %all-gather.6.cloned.1.call-done = bf16[1024,5120]{1,0:T(8,128)(2,1)} async-done(((bf16[1024,1280]{1,0:T(8,128)(2,1)}), bf16[1024,5120]{1,0:T(8,128)(2,1)}) %all-gather.6.cloned.1.call-update) | async-done | bytes 10485776 | tf_op jit(solution)/shard_map/all_gather | solution.py:70
  324.1 9.8 %fusion.16 = bf16[1024,512]{1,0:T(8,128)(2,1)S(1)} fusion(bf16[1024,5120]{1,0:T(8,128)(2,1)} %all-gather.6.cloned.1.call-done, bf16[1,5120,512]{2,1,0:T(8,128)(2,1)} %param.15), kind=kOutput, calls=%fused_computation.32 | convolution fusion | flops 5369233408 | bytes 16777216 | tf_op jit(solution)/shard_map/dot_general | solution.py:69
  334.0 0.3 broadcast_in_dim.111
  334.2 2.5 scatter_fusion
  336.7 1.3 copy-done.1
  338.1 9.6 %all-to-all-start = ((bf16[16,8,16,512]{3,2,1,0:T(8,128)(2,1)}), bf16[16,8,16,512]{3,2,1,0:T(8,128)(2,1)S(1)}, u32[]{:S(2)}, u32[]{:S(2)}) async-start(bf16[16,8,16,512]{3,2,1,0:T(8,128)(2,1)} %bitcast.136), calls=%async_computation | async-start | bytes 4194304 | tf_op jit(solution)/shard_map/all_to_all | solution.py:91
  347.7 0.1 convert_reduce_fusion
  347.8 4.2 copy.103
  352.0 4.5 scatter_custom_fusion.1
  356.5 12.6 %gather_fusion = s32[2048]{0:T(1024)S(1)} fusion(s32[128]{0:T(128)S(1)} %scatter_custom_fusion.1, s32[2048]{0:T(1024)S(1)} %broadcast_clamp_fusion), kind=kCustom, calls=%fused_computation | custom fusion | bytes 24576 | tf_op jit(solution)/shard_map/jit(_take)/gather | solution.py:99
  369.3 1.6 select_reduce_fusion.2
  370.9 7.5 %all-to-all-done = bf16[16,8,16,512]{3,2,1,0:T(8,128)(2,1)S(1)} async-done(((bf16[16,8,16,512]{3,2,1,0:T(8,128)(2,1)}), bf16[16,8,16,512]{3,2,1,0:T(8,128)(2,1)S(1)}, u32[]{:S(2)}, u32[]{:S(2)}) %all-to-all-start) | async-done | bytes 2097184 | tf_op jit(solution)/shard_map/all_to_all | solution.py:91
  378.4 2.0 reshape_reshape.3
  380.5 2.7 fusion.50
  383.1 0.7 select_reduce_fusion
  383.9 0.7 fusion.48
  384.6 0.1 copy-done.2
  384.7 1.1 convolution_bitcast_fusion.2
  385.8 1.2 fusion.23
  387.0 0.6 copy.115
  387.7 0.4 select_reduce_fusion.3
  388.1 0.3 fusion.29
  388.4 21.4 %all-gather.1 = f32[64,4,2,4]{3,1,2,0:T(4,128)S(1)} all-gather(f32[4,4,2,4]{3,1,2,0:T(4,128)S(1)} %copy_add_fusion), channel_id=3, replica_groups=mesh['section'=4,'ctx'=16,'tp'=4] {'ctx'}, dimensions={0}, use_global_device_ids=true | all-gather | bytes 8704 | tf_op jit(solution)/shard_map/all_gather | solution.py:24
  409.8 23.6 %all-gather = f32[64,4,2,4]{3,1,2,0:T(4,128)S(1)} all-gather(f32[4,4,2,4]{3,1,2,0:T(4,128)S(1)} %copy_maximum_fusion), channel_id=2, replica_groups=mesh['section'=4,'ctx'=16,'tp'=4] {'ctx'}, dimensions={0}, use_global_device_ids=true | all-gather | bytes 8704 | tf_op jit(solution)/shard_map/all_gather | solution.py:24
  433.5 0.8 slice.54
  434.4 17.5 %while.20 = (s32[]{:T(128)}, f32[4,4,2,4]{3,2,1,0:T(2,128)S(1)}, f32[4,4,2,4]{3,2,1,0:T(2,128)S(1)}, f32[4,4,2,4,128]{4,3,2,1,0:T(4,128)S(1)}, f32[16,4,4,2,4]{4...) while((s32[]{:T(128)}, f32[4,4,2,4]{3,2,1,0:T(2,128)S(1)}, ...), condition=%wide.region_13.14_spmd, body=%wide.region_12.13_spmd.sunk | while | flops 49925 | bytes 203927 | solution.py:29
  434.4 1.1 fusion.56
  435.6 1.1 fusion.56
  436.8 1.1 fusion.56
  437.9 1.1 fusion.56
  439.1 1.1 fusion.56
  440.3 1.1 fusion.56
  441.4 1.1 fusion.56
  442.6 1.1 fusion.56
  443.8 1.1 fusion.56
  444.9 1.1 fusion.56
  446.1 1.1 fusion.56
  447.3 1.1 fusion.56
  448.4 1.1 fusion.56
  449.6 1.1 fusion.56
  450.8 1.1 fusion.56
  451.9 0.1 fusion.33
  452.0 0.4 fusion.24
  452.4 0.6 convert_element_type.71
  453.1 1.3 copy.207
  (77 shorter events, 1.7 us)
Async XLA Ops:
  7.2 317.0 %all-gather.6.cloned.1.call-start = ((), (), s32[]{:S(2)}) async-start(), calls=%async_computation.1 | async-start | bytes 13107200 | tf_op jit(solution)/shard_map/all_gather | solution.py:70
  7.2 6.6 %collective-permute-start = (bf16[1024,1280]{1,0:T(8,128)(2,1)}, bf16[1024,1280]{1,0:T(8,128)(2,1)}, u32[]{:S(2)}, u32[]{:S(2)}) collective-permute-start(bf16[1024,1280]{1,0:T(8,128)(2,1)} %bitcast.134), channel_id=1, source_target_pairs={{0,64},{64,128},{128,192},{1,65},{65,129},{129,193},{2,66},{66,130... | collective-permute-start | bytes 7864328 | tf_op jit(solution)/shard_map/ppermute | solution.py:20
  10.5 41.1 %copy-start = (bf16[1,1024,1280]{2,1,0:T(8,128)(2,1)S(1)}, bf16[1,1024,1280]{2,1,0:T(8,128)(2,1)}, u32[]{:S(2)}) copy-start(bf16[1,1024,1280]{2,1,0:T(8,128)(2,1)} %param.13) | copy-start | bytes 7864324
  18.6 33.0 %collective-permute-start.1 = (bf16[1024,1280]{1,0:T(8,128)(2,1)}, bf16[1024,1280]{1,0:T(8,128)(2,1)}, u32[]{:S(2)}, u32[]{:S(2)}) collective-permute-start(bf16[1024,1280]{1,0:T(8,128)(2,1)} %fusion.12), channel_id=1, source_target_pairs={{0,64},{64,128},{128,192},{1,65},{65,129},{129,193},{2,66},{66,130... | collective-permute-start | bytes 7864328 | tf_op jit(solution)/shard_map/ppermute | solution.py:20
  48.3 38.2 %copy-start.6 = (bf16[1,1280]{1,0:T(2,128)(2,1)S(1)}, bf16[1,1280]{1,0:T(2,128)(2,1)}, u32[]{:S(2)}) copy-start(bf16[1,1280]{1,0:T(2,128)(2,1)} %param.14) | copy-start | bytes 7684
  56.6 33.3 %collective-permute-start.2 = (bf16[1024,1280]{1,0:T(8,128)(2,1)}, bf16[1024,1280]{1,0:T(8,128)(2,1)}, u32[]{:S(2)}, u32[]{:S(2)}) collective-permute-start(bf16[1024,1280]{1,0:T(8,128)(2,1)} %fusion.14), channel_id=1, source_target_pairs={{0,64},{64,128},{128,192},{1,65},{65,129},{129,193},{2,66},{66,130... | collective-permute-start | bytes 7864328 | tf_op jit(solution)/shard_map/ppermute | solution.py:20
  110.3 0.7 copy-start.5
  110.3 3.2 copy-start.9
  110.3 3.5 copy-start.3
  336.7 1.3 copy-start.1
  338.1 9.8 %copy-start.4 = (bf16[1,4,4,1024]{3,2,1,0:T(4,128)(2,1)S(1)}, bf16[1,4,4,1024]{3,2,1,0:T(4,128)(2,1)}, u32[]{:S(2)}) copy-start(bf16[1,4,4,1024]{3,2,1,0:T(4,128)(2,1)} %param.20) | copy-start | bytes 98308
  338.1 40.4 %all-to-all-start = ((bf16[16,8,16,512]{3,2,1,0:T(8,128)(2,1)}), bf16[16,8,16,512]{3,2,1,0:T(8,128)(2,1)S(1)}, u32[]{:S(2)}, u32[]{:S(2)}) async-start(bf16[16,8,16,512]{3,2,1,0:T(8,128)(2,1)} %bitcast.136), calls=%async_computation | async-start | bytes 4194304 | tf_op jit(solution)/shard_map/all_to_all | solution.py:91
  347.7 85.8 %all-gather.8.cloned.1.call-start = ((), (), s32[]{:S(2)}) async-start(), calls=%async_computation.2 | async-start | bytes 1114112 | tf_op jit(solution)/shard_map/all_gather | solution.py:24
  356.5 12.7 %copy-start.7 = (s32[4]{0:T(128)S(1)}, s32[4]{0:T(128)}, u32[]{:S(2)}) copy-start(s32[4]{0:T(128)} %param.18) | copy-start | bytes 52
  383.1 1.6 copy-start.2
  385.8 1.9 copy-start.8
Sparse Core Ops, SparseCore 0:
  110.5 213.6 all-gather.5
  387.8 43.4 all-gather.7
where the time goes:
time: 463 us; the launch traced here: 461 us
  waiting for transfers between devices  228 us (49%)
  starting transfers between devices  72.6 us (16%)
  blocking collectives  56.3 us (12%)
  other arithmetic  39.8 us (9%)
  local copies, waits for them, and re-layouts  34.8 us (8%)
  matrix products  15.2 us (3%)
  between operations  14.3 us (3%)
    all_gather x1, waiting for transfers between devices, per_device(): lax.all_gather(normed, 'tp', axis=1, tiled=True)  210 us
    ppermute x3, starting transfers between devices, from_behind(): return lax.ppermute(array, axis, pairs)  62.9 us
    all_gather x2, blocking collectives, joined(): gathered = jax.tree.map(lambda a: lax.all_gather(a, axis), part)  45.1 us
    add x15, other arithmetic, combine(): first[2] * first_factor[..., None] + second[2] * second_factor[..., None]  16.2 us
    gather x1, local copies, waits for them, and re-layouts, per_device(): jnp.repeat(slot_session, PAGE, total_repeat_length=n_ctx * capacity * PAGE)  12.6 us
    psum x1, blocking collectives, per_device(): sums = lax.psum(jnp.sum(wide * wide, axis=1, keepdims=True), 'tp')  11.2 us
    ppermute x3, waiting for transfers between devices, from_behind(): return lax.ppermute(array, axis, pairs)  9.96 us
    dot_general x1, matrix products, per_device(): jnp.dot(lax.all_gather(normed, 'tp', axis=1, tiled=True), weight, preferr...  9.82 us
  transfers between devices with their start and end apart: 6, of which 5 were waited for; matrix products, arithmetic and copies ran while one was open for 6% of the time, Pallas kernels for 0%

commit v1 on v0

v1 whole, which is shorter than its diff:
```python
import functools

import jax
import jax.numpy as jnp
from jax import lax
from jax.experimental import pallas as pl
from jax.experimental.pallas import tpu as pltpu
from jax.sharding import PartitionSpec as P

D = 5120
HEAD_DIM = 128
SESSIONS = 4
STEPS = 4
PAGE = 16
SIDE = 4

epsilon = 1e-05
floor_value = -1e30
bf16 = jnp.bfloat16
f32 = jnp.float32
VMEM = pl.BlockSpec(memory_space=pltpu.VMEM)
SMEM = pl.BlockSpec(memory_space=pltpu.SMEM)
ANY = pl.BlockSpec(memory_space=pl.ANY)
MEBI = 1024 * 1024
NO_COST = pl.CostEstimate(flops=0, bytes_accessed=0, transcendentals=0)


def shift_tp(array, by):
    peers = lax.axis_size("tp")
    return lax.ppermute(array, "tp", [(i, (i + by) % peers) for i in range(peers)])


def from_x(array, by):
    pairs = [(((i // SIDE + by) % SIDE) * SIDE + i % SIDE, i) for i in range(SIDE * SIDE)]
    return lax.ppermute(array, "ctx", pairs)


def from_y(array, by):
    pairs = [((i // SIDE) * SIDE + (i % SIDE + by) % SIDE, i) for i in range(SIDE * SIDE)]
    return lax.ppermute(array, "ctx", pairs)


def added(first, second):
    return (first.astype(f32) + second.astype(f32)).astype(bf16)


def add_kernel(first, second, *refs):
    refs[-1][...] = added(first[...], second[...])


def add_after(first, second, *after):
    rows, columns = first.shape
    block = pl.BlockSpec((rows // 4, columns), lambda i: (i, 0))
    return pl.pallas_call(
        add_kernel,
        grid=(4,),
        out_shape=jax.ShapeDtypeStruct(first.shape, bf16),
        in_specs=[block, block] + [ANY] * len(after),
        out_specs=block,
        compiler_params=pltpu.CompilerParams(vmem_limit_bytes=8 * MEBI),
        cost_estimate=NO_COST,
    )(first, second, *after)


def nothing(*refs):
    pass


def tied(array, *after):
    return pl.pallas_call(
        nothing,
        out_shape=jax.ShapeDtypeStruct(array.shape, array.dtype),
        in_specs=[ANY] * (1 + len(after)),
        out_specs=ANY,
        input_output_aliases={0: 0},
        cost_estimate=NO_COST,
    )(array, *after)


def pieces_kernel(place, weight, one, three, far, sems):
    x, y, rank = place[0], place[1], place[2]
    rows = one.shape[0]
    features = rows * SIDE
    copies = []
    for n, (out, behind, row, column) in enumerate(((one, 1, y, x), (three, 3, y, x), (far, 2, x, y))):
        start = lax.rem(rank + SIDE - behind, SIDE) * features + row * rows
        copies.append(
            pltpu.make_async_copy(
                weight.at[
                    pl.ds(pl.multiple_of(start, rows), rows),
                    pl.ds(pl.multiple_of(column * HEAD_DIM, HEAD_DIM), HEAD_DIM),
                ],
                out,
                sems.at[n],
            )
        )
    for copy in copies:
        copy.start()
    for copy in copies:
        copy.wait()


def rows_kernel(axis, place, *refs):
    out = refs[-1]
    rows = refs[0].shape[-2]
    for k in range(SIDE):
        start = pl.multiple_of(lax.rem(place[axis] + k, SIDE) * rows, rows)
        if len(out.shape) == 2:
            out[pl.ds(start, rows), :] = refs[k][...]
        else:
            out[:, pl.ds(start, rows), :] = refs[k][...]


def columns_kernel(place, *refs):
    out = refs[-1]
    half = out.shape[1] // 2
    for k in range(SIDE):
        start = lax.rem(place[0] + k, SIDE) * HEAD_DIM
        for n in range(2):
            out[:, pl.ds(pl.multiple_of(n * half + start, HEAD_DIM), HEAD_DIM)] = refs[k][n]


def dot_rows(hs, weight, start):
    return jnp.dot(hs[start : start + 256, :], weight, preferred_element_type=f32)


def far_kernel(where, hs, *refs):
    parts, (low, high), held, sems = refs[:SIDE], refs[SIDE : SIDE + 2], refs[-2], refs[-1]
    copies = []
    for k in range(SIDE):
        column = pl.multiple_of(lax.rem(where[1] + k, SIDE) * HEAD_DIM, HEAD_DIM)
        copies.append(pltpu.make_async_copy(parts[k], held.at[:, pl.ds(column, HEAD_DIM)], sems.at[k]))
    for copy in copies:
        copy.start()
    for copy in copies:
        copy.wait()
    cut = low.shape[0]
    for start in range(0, hs.shape[0], 256):
        out, at = (low, start) if start < cut else (high, start - cut)
        out[at : at + 256, :] = dot_rows(hs, held[...], start).astype(bf16)


def own_kernel(hs, weight, place, after, *refs):
    outs, held, sem = refs[:-2], refs[-2], refs[-1]
    rows = held.shape[0]
    copy = pltpu.make_async_copy(weight.at[pl.ds(pl.multiple_of(place[2] * rows, rows), rows)], held, sem)
    copy.start()
    copy.wait()
    for start in range(0, hs.shape[0], 256):
        column = 0
        for out in outs:
            width = out.shape[1]
            out[start : start + 256, :] = dot_rows(hs, held[:, column : column + width], start)
            column += width


def near_kernel(first, widths, hs, weight, far_low, far_high, *refs):
    outs = refs[-2 * len(widths) :]
    columns = far_low.shape[1]
    cut = far_low.shape[0]
    for start in range(0, hs.shape[0], 256):
        block = slice(start, start + 256)
        column = first
        for n, width in enumerate(widths):
            cols = slice(column, column + width)
            ahead = dot_rows(hs, weight[:, cols], start)
            behind = dot_rows(hs, weight[:, columns + column : columns + column + width], start)
            if start < cut:
                ahead = ahead + far_low[block, cols].astype(f32)
            else:
                behind = behind + far_high[start - cut : start - cut + 256, cols].astype(f32)
            outs[2 * n][block, :] = ahead.astype(bf16)
            outs[2 * n + 1][block, :] = behind.astype(bf16)
            column += width


def lay_pages(source, fresh, payload):
    owners, capacity = payload.shape[0], source.shape[0] // payload.shape[0]

    def place(owner, carry):
        for r in range(capacity):
            page = source[owner * capacity + r]

            @pl.when(page >= 0)
            def _():
                payload[owner, r] = fresh[pl.ds(pl.multiple_of(page * PAGE, PAGE), PAGE), :]

            @pl.when(page < 0)
            def _():
                payload[owner, r] = jnp.zeros(payload.shape[2:], bf16)

        return carry

    lax.fori_loop(0, owners, place, 0)


def sum_rows(own, ahead, behind, scale, fresh):
    for start in range(0, fresh.shape[0], 128):
        block = slice(start, start + 128)
        total = own[block, :] + ahead[block, :].astype(f32) + behind[block, :].astype(f32)
        fresh[block, :] = (total * scale[block, :1]).astype(bf16)


def keys_kernel(source, own, ahead, behind, scale, fresh, payload):
    sum_rows(own, ahead, behind, scale, fresh)
    lay_pages(source, fresh, payload)


def values_kernel(
    j, where, ends, source, own, ahead, behind, scale, keys, queries, peak, total, mixed, *refs
):
    payload, fresh = refs[-2:]
    sum_rows(own, ahead, behind, scale, fresh)
    lay_pages(source, fresh, payload)
    rows = peak.shape[0] // (keys.shape[1] // HEAD_DIM)
    count = fresh.shape[0]
    group = rows // (SESSIONS * STEPS)
    ctx = where[0] * SIDE + where[1]
    query = head_queries(queries, j, group)
    session, step, key = row_ids(rows, count)
    page = key // PAGE + ctx * (count // PAGE)
    owner_session = jnp.zeros_like(page)
    for s in range(SESSIONS):
        owner_session = owner_session + (ends[s] <= page).astype(jnp.int32)
    block = slice(j * rows, (j + 1) * rows)
    state = (peak[block, :1], total[block, :1], mixed[block, :])
    state = attend(
        state, query, keys[:, j * HEAD_DIM : (j + 1) * HEAD_DIM], fresh[...], session == owner_session
    )
    some = state[1] > 0.0
    divisor = jnp.where(some, state[1], 1.0)
    level = jnp.where(some, state[0] + jnp.log(divisor), floor_value)
    level = jnp.broadcast_to(level, (rows, HEAD_DIM))
    level = jnp.concatenate([level] * (HEAD_DIM // rows), axis=0).T[:PAGE]
    high = level.astype(bf16).astype(f32)
    middle = (level - high).astype(bf16).astype(f32)
    low = level - high - middle
    line = lax.broadcasted_iota(jnp.int32, level.shape, 0)
    terms = jnp.where(line == 0, high, jnp.where(line == 1, middle, jnp.where(line == 2, low, 0.0)))
    terms = terms.astype(bf16)
    part = (state[2] / divisor).astype(bf16).reshape(rows // PAGE, PAGE, HEAD_DIM)
    first = payload.shape[1] - rows // PAGE - 1

    def spread(owner, carry):
        payload[owner, first : first + rows // PAGE] = part
        payload[owner, first + rows // PAGE] = terms
        return carry

    lax.fori_loop(0, payload.shape[0], spread, 0)


def last_kernel(*refs):
    key_pages, value_parts, pages, out = refs[0], refs[1:-2], refs[-2], refs[-1]
    owners, capacity, _, key_cols = key_pages.shape
    for i in range(owners):
        slots = slice(i * capacity, (i + 1) * capacity)
        pages[slots, :, :key_cols] = key_pages[i]
        for j, part in enumerate(value_parts):
            column = key_cols + j * HEAD_DIM
            pages[slots, :, column : column + HEAD_DIM] = part[i, :capacity]
    steps = SESSIONS * STEPS
    for j, part in enumerate(value_parts):
        blocks = part.shape[1] - capacity - 1
        rows = blocks * PAGE
        line = lax.broadcasted_iota(jnp.int32, (owners, HEAD_DIM), 0)
        level = jnp.zeros((owners, HEAD_DIM), f32)
        for i in range(owners):
            terms = part[i, capacity + blocks].astype(f32)
            level = jnp.where(line == i, terms[0:1] + terms[1:2] + terms[2:3], level)
        share = jnp.exp(level - jnp.max(level, axis=0, keepdims=True))
        share = share / jnp.sum(share, axis=0, keepdims=True)
        share = jnp.concatenate([share, jnp.zeros((HEAD_DIM - owners, HEAD_DIM), f32)], axis=0).T
        total = jnp.zeros((rows, HEAD_DIM), f32)
        for i in range(owners):
            total = total + share[:rows, i : i + 1] * part[i, capacity : capacity + blocks].reshape(
                rows, HEAD_DIM
            ).astype(f32)
        result = total.astype(bf16)
        for g in range(rows // steps):
            column = (j * (rows // steps) + g) * HEAD_DIM
            out[:, column : column + HEAD_DIM] = result[g * steps : (g + 1) * steps, :]


def head_queries(queries, j, group):
    return jnp.concatenate(
        [queries[:, (j * group + g) * HEAD_DIM : (j * group + g + 1) * HEAD_DIM] for g in range(group)], axis=0
    )


def attend(state, query, keys, values, mask):
    peak, total, mixed = state
    scores = lax.dot_general(query, keys, (((1,), (1,)), ((), ())), preferred_element_type=f32)
    scores = jnp.where(mask, scores * HEAD_DIM ** (-0.5), floor_value)
    top = jnp.maximum(peak, jnp.max(scores, axis=1, keepdims=True))
    weights = jnp.where(mask, jnp.exp(scores - top), 0.0)
    factor = jnp.exp(peak - top)
    total = total * factor + jnp.sum(weights, axis=1, keepdims=True)
    mixed = mixed * factor + jnp.dot(weights.astype(bf16), values, preferred_element_type=f32)
    return top, total, mixed


def row_ids(rows, length):
    row = lax.broadcasted_iota(jnp.int32, (rows, length), 0) % (SESSIONS * STEPS)
    key = lax.broadcasted_iota(jnp.int32, (rows, length), 1)
    return row // STEPS, row % STEPS, key


def cache_kernel(where, lengths, queries, cache, new, after, peak_out, total_out, mixed_out):
    per_group = cache.shape[2] // (2 * HEAD_DIM)
    group = queries.shape[1] // (HEAD_DIM * per_group)
    rows = group * SESSIONS * STEPS
    local = cache.shape[1]
    ctx = where[0] * SIDE + where[1]
    for j in range(per_group):
        query = head_queries(queries, j, group)
        key_cols = slice(j * HEAD_DIM, (j + 1) * HEAD_DIM)
        value_cols = slice((per_group + j) * HEAD_DIM, (per_group + j + 1) * HEAD_DIM)
        state = (
            jnp.full((rows, 1), floor_value, f32),
            jnp.zeros((rows, 1), f32),
            jnp.zeros((rows, HEAD_DIM), f32),
        )
        for s in range(SESSIONS):
            session, step, key = row_ids(rows, local)
            mask = (session == s) & (key + ctx * local < lengths[s])
            state = attend(state, query, cache[s, :, key_cols], cache[s, :, value_cols], mask)
        session, step, key = row_ids(rows, new.shape[0])
        mask = (session == key // STEPS) & (key % STEPS <= step) & (ctx == 0)
        state = attend(state, query, new[:, key_cols], new[:, value_cols], mask)
        block = slice(j * rows, (j + 1) * rows)
        peak_out[block, :] = jnp.broadcast_to(state[0], (rows, HEAD_DIM))
        total_out[block, :] = jnp.broadcast_to(state[1], (rows, HEAD_DIM))
        mixed_out[block, :] = state[2]


def call(kernel, out_shape, in_specs, *operands, vmem=16, scratch=()):
    return pl.pallas_call(
        kernel,
        out_shape=out_shape,
        in_specs=in_specs,
        out_specs=jax.tree.map(lambda _: VMEM, out_shape),
        scratch_shapes=scratch,
        compiler_params=pltpu.CompilerParams(vmem_limit_bytes=vmem * MEBI),
        cost_estimate=NO_COST,
    )(*operands)


def per_device(
    layer_inputs, norm_gain, kv_weight, span_pages, page_owner, cache_len, cache_kv, queries, new_kv
):
    n_ctx = lax.axis_size("ctx")
    ctx_index = lax.axis_index("ctx")
    tp_index = lax.axis_index("tp")
    place = jnp.stack([ctx_index // SIDE, ctx_index % SIDE, tp_index]).astype(jnp.int32)
    own_part = layer_inputs[0]
    row_count, features = own_part.shape
    weight = kv_weight[0]
    kv_cols = weight.shape[1]
    shape = jax.ShapeDtypeStruct

    part_rows = features // SIDE
    one, three, band = call(
        pieces_kernel,
        [shape((part_rows, HEAD_DIM), bf16)] * 3,
        [SMEM, ANY],
        place,
        weight,
        scratch=[pltpu.SemaphoreType.DMA((3,))],
    )
    band = shift_tp(band, 2)
    near = jnp.stack([shift_tp(one, -1), shift_tp(three, 1)])
    far_column = call(
        functools.partial(rows_kernel, 0),
        shape((features, HEAD_DIM), bf16),
        [SMEM] + [VMEM] * SIDE,
        place,
        band,
        *[from_x(band, k) for k in range(1, SIDE)],
    )
    near_column = call(
        functools.partial(rows_kernel, 1),
        shape((2, features, HEAD_DIM), bf16),
        [SMEM] + [VMEM] * SIDE,
        place,
        near,
        *[from_y(near, k) for k in range(1, SIDE)],
    )
    far_parts = [far_column] + [from_y(far_column, k) for k in range(1, SIDE)]
    near_weight = call(
        columns_kernel,
        shape((features, 2 * kv_cols), bf16),
        [SMEM] + [VMEM] * SIDE,
        place,
        near_column,
        *[from_x(near_column, k) for k in range(1, SIDE)],
    )

    inner = lax.ppermute(own_part, "section", [(0, 1), (2, 3)])
    crossed = lax.ppermute(add_after(inner, own_part, band, near), "section", [(1, 2)])
    crossed = tied(crossed, near_column, *far_parts)
    passed = lax.ppermute(crossed, "section", [(2, 3)])

    arrived = (inner.astype(f32) + crossed.astype(f32) + passed.astype(f32)).astype(bf16)
    hidden = added(arrived, own_part)
    wide = hidden.astype(f32)
    hs = (wide * norm_gain[0].astype(f32)).astype(bf16)
    squares = jnp.sum(wide * wide, axis=1).reshape(-1, HEAD_DIM)

    cut = row_count // 2
    far_low, far_high = call(
        far_kernel,
        [shape((cut, kv_cols), bf16), shape((row_count - cut, kv_cols), bf16)],
        [SMEM, VMEM] + [ANY] * SIDE,
        place,
        hs,
        *far_parts,
        scratch=[pltpu.VMEM((features, kv_cols), bf16), pltpu.SemaphoreType.DMA((SIDE,))],
    )
    key_cols = kv_cols // 2
    value_cols = [HEAD_DIM] * (key_cols // HEAD_DIM)
    own = call(
        own_kernel,
        [shape((row_count, width), f32) for width in [key_cols] + value_cols],
        [VMEM, ANY, SMEM, ANY],
        hs,
        weight,
        place,
        far_low,
        scratch=[pltpu.VMEM((features, kv_cols), bf16), pltpu.SemaphoreType.DMA],
    )
    squares = squares + shift_tp(squares, 1) + shift_tp(squares, -1) + shift_tp(squares, 2)
    scale = jnp.broadcast_to(
        lax.rsqrt(squares / D + epsilon).reshape(row_count, 1), (row_count, HEAD_DIM)
    )
    query = queries[0].reshape(SESSIONS * STEPS, -1)
    new = jnp.pad(new_kv[0].reshape(SESSIONS * STEPS, kv_cols), ((0, HEAD_DIM - SESSIONS * STEPS), (0, 0)))
    state_shape = shape((query.shape[1] // HEAD_DIM * SESSIONS * STEPS, HEAD_DIM), f32)
    state = call(
        cache_kernel,
        [state_shape] * 3,
        [SMEM, SMEM, VMEM, VMEM, VMEM, ANY],
        place,
        cache_len,
        query,
        cache_kv[0],
        new,
        far_low,
    )
    passing = (shift_tp(far_low, 1), shift_tp(far_high, -1))
    key_sums = call(
        functools.partial(near_kernel, 0, [key_cols]),
        [shape((row_count, key_cols), bf16)] * 2,
        [VMEM] * 4 + [ANY] * 4,
        hs,
        near_weight,
        *passing,
        *state,
        own[0],
    )
    value_sums = call(
        functools.partial(near_kernel, key_cols, value_cols),
        [shape((row_count, HEAD_DIM), bf16)] * (2 * len(value_cols)),
        [VMEM] * 4 + [ANY],
        hs,
        near_weight,
        *passing,
        key_sums[0],
    )
    key_sums = (shift_tp(key_sums[0], 1), shift_tp(key_sums[1], -1))
    value_sums = [shift_tp(part, 1 if n % 2 == 0 else -1) for n, part in enumerate(value_sums)]

    pages_dev = row_count // PAGE
    capacity = max(2, 2 * pages_dev // n_ctx)
    owner = lax.dynamic_slice_in_dim(page_owner[:, 0], ctx_index * pages_dev, pages_dev)
    order = jnp.arange(pages_dev, dtype=jnp.int32)
    earlier = (owner[:, None] == owner[None, :]) & (order[None, :] < order[:, None])
    target = owner * capacity + jnp.sum(earlier.astype(jnp.int32), axis=1)
    slots = jnp.arange(n_ctx * capacity, dtype=jnp.int32)
    source = jnp.max(jnp.where(target[None, :] == slots[:, None], order[None, :], -1), axis=1)
    ends = jnp.cumsum(span_pages)

    fresh_keys, key_pages = call(
        keys_kernel,
        [shape((row_count, key_cols), bf16), shape((n_ctx, capacity, PAGE, key_cols), bf16)],
        [SMEM] + [VMEM] * 4,
        source,
        own[0],
        *key_sums,
        scale,
    )
    key_pages = lax.all_to_all(key_pages, "ctx", split_axis=0, concat_axis=0, tiled=True)
    value_parts = []
    for j in range(len(value_cols)):
        rows = state_shape.shape[0] // len(value_cols)
        payload = call(
            functools.partial(values_kernel, j),
            shape((n_ctx, capacity + rows // PAGE + 1, PAGE, HEAD_DIM), bf16),
            [SMEM] * 3 + [VMEM] * 9 + [ANY] * j,
            place,
            ends,
            source,
            own[1 + j],
            value_sums[2 * j],
            value_sums[2 * j + 1],
            scale,
            fresh_keys,
            query,
            *state,
            *[key_pages] * j,
            scratch=[pltpu.VMEM((row_count, HEAD_DIM), bf16)],
        )
        value_parts.append(lax.all_to_all(payload, "ctx", split_axis=0, concat_axis=0, tiled=True))
    page_store, attention = call(
        last_kernel,
        [shape((n_ctx * capacity, PAGE, kv_cols), bf16), shape(query.shape, bf16)],
        [VMEM] * (1 + len(value_parts)),
        key_pages,
        *value_parts,
    )
    return (page_store[None], attention.reshape(1, SESSIONS, STEPS, -1))


def solution(mesh):
    return jax.shard_map(
        per_device,
        mesh=mesh,
        in_specs=(
            P("section", "ctx", "tp"),
            P("section", "tp"),
            P("section", None, "tp"),
            P(),
            P(),
            P(),
            P("section", None, "ctx", "tp"),
            P("section", None, None, "tp"),
            P("section", None, None, "tp"),
        ),
        out_specs=(P("section", "ctx", None, "tp"), P("section", None, None, "tp")),
        check_vma=False,
    )
```

time: 463 us -> 227 us (0.49)
  waiting for transfers between devices: 228 us -> 80.4 us
  blocking collectives: 56.3 us -> 19.1 us
  Pallas kernels: 0 us -> 36.6 us
  other arithmetic: 39.8 us -> 6.13 us
  matrix products: 15.2 us -> 0 us
  local copies, waits for them, and re-layouts: 34.8 us -> 20.8 us
  starting transfers between devices: 72.6 us -> 59.1 us
  between operations: 14.3 us -> 1.09 us
    all_gather x2 -> x0, waiting for transfers between devices: 210 us -> none  [the longest x1 210 us: per_device(): lax.all_gather(normed, 'tp', axis=1, tiled=True)]
    ppermute x3 -> x29, waiting for transfers between devices: 9.96 us -> 80.4 us  [the longest x14 38.1 us: shift_tp(): lax.ppermute(array, 'tp', [(i, (i + by) % peers) for i in range(peers)])]
    all_gather x2 -> x0, blocking collectives: 45.1 us -> none  [joined(): gathered = jax.tree.map(lambda a: lax.all_gather(a, axis), part)]
    pallas_call x0 -> x15, Pallas kernels: none -> 36.6 us  [the longest x13 33.9 us: call(): pl.pallas_call(kernel, out_shape=out_shape, in_specs=in_specs, out_specs=...]
    all_to_all x0 -> x1, blocking collectives: none -> 19.1 us  [per_device(): lax.all_to_all(payload, 'ctx', split_axis=0, concat_axis=0, tiled=True)]
    add x33 -> x1, other arithmetic: 16.9 us -> 0.73 us  [per_device(): target = owner * capacity + jnp.sum(earlier.astype(jnp.int32), axis=1)]
    dot_general x7 -> x0, matrix products: 15.2 us -> none  [the longest x1 9.82 us: per_device(): jnp.dot(lax.all_gather(normed, 'tp', axis=1, tiled=True), weight, preferr...]
    ppermute x3 -> x29, starting transfers between devices: 62.9 us -> 47.9 us  [the longest x14 26.4 us: shift_tp(): lax.ppermute(array, 'tp', [(i, (i + by) % peers) for i in range(peers)])]
  transfers between devices with their start and end apart: 6 -> 31, of which waited for: 5 -> 13; matrix products, arithmetic and copies ran while one was open for 6% -> 3% of each run, Pallas kernels for 0% -> 11%
where the time goes in v1:
time: 227 us; the launch traced here: 223 us
  waiting for transfers between devices  80.4 us (35%)
  starting transfers between devices  59.1 us (26%)
  Pallas kernels  36.6 us (16%)
  local copies, waits for them, and re-layouts  20.8 us (9%)
  blocking collectives  19.1 us (8%)
  other arithmetic  6.13 us (3%)
    ppermute x14, waiting for transfers between devices, shift_tp(): lax.ppermute(array, 'tp', [(i, (i + by) % peers) for i in range(peers)])  38.1 us
    pallas_call x13, Pallas kernels, call(): pl.pallas_call(kernel, out_shape=out_shape, in_specs=in_specs, out_specs=...  33.9 us
    ppermute x14, starting transfers between devices, shift_tp(): lax.ppermute(array, 'tp', [(i, (i + by) % peers) for i in range(peers)])  26.4 us
    ppermute x6, waiting for transfers between devices, from_x(): return lax.ppermute(array, 'ctx', pairs)  24.3 us
    unnamed x74, local copies, waits for them, and re-layouts  19.2 us
    all_to_all x1, blocking collectives, per_device(): lax.all_to_all(payload, 'ctx', split_axis=0, concat_axis=0, tiled=True)  19.1 us
    ppermute x6, waiting for transfers between devices, from_y(): return lax.ppermute(array, 'ctx', pairs)  18 us
    ppermute x6, starting transfers between devices, from_y(): return lax.ppermute(array, 'ctx', pairs)  7.95 us
  transfers between devices with their start and end apart: 31, of which 13 were waited for; matrix products, arithmetic and copies ran while one was open for 3% of the time, Pallas kernels for 11%

profile of v1, /device:TPU:64, one launch (start us, length us, event | category | flops | bytes accessed | tf_op | source)
XLA Modules:
  0.0 223.2 jit_solution(7676413841722451728)
XLA Ops:
  0.6 3.2 %collective-permute-start = (bf16[1024,1280]{1,0:T(8,128)(2,1)}, bf16[1024,1280]{1,0:T(8,128)(2,1)}, u32[]{:S(2)}, u32[]{:S(2)}) collective-permute-start(bf16[1024,1280]{1,0:T(8,128)(2,1)} %bitcast.23), channel_id=1, source_target_pairs={{0,64},{128,192},{1,65},{129,193},{2,66},{130,194},{3,67},{131,195... | collective-permute-start | bytes 7864328 | tf_op jit(solution)/shard_map/ppermute | solution.py:398
  3.9 2.5 %copy-done.2 = bf16[1,5120,512]{2,1,0:T(8,128)(2,1)S(1)} copy-done((bf16[1,5120,512]{2,1,0:T(8,128)(2,1)S(1)}, bf16[1,5120,512]{2,1,0:T(8,128)(2,1)}, u32[]{:S(2)}) %copy-start.2) | copy-done | bytes 5242904
  7.1 4.6 %collective-permute-start.3 = (bf16[320,128]{1,0:T(8,128)(2,1)S(1)}, bf16[320,128]{1,0:T(8,128)(2,1)S(1)}, u32[]{:S(2)}, u32[]{:S(2)}) collective-permute-start(bf16[320,128]{1,0:T(8,128)(2,1)S(1)} %get-tuple-element.25), channel_id=1, source_target_pairs={{0,1},{1,2},{2,3},{3,0},{4,5},{5,6},{6,7},{7,4},{8,9},{9,10},{10,1... | collective-permute-start | bytes 245768 | tf_op jit(solution)/shard_map/ppermute | solution.py:30
  11.6 3.8 %collective-permute-start.1 = (bf16[320,128]{1,0:T(8,128)(2,1)S(1)}, bf16[320,128]{1,0:T(8,128)(2,1)S(1)}, u32[]{:S(2)}, u32[]{:S(2)}) collective-permute-start(bf16[320,128]{1,0:T(8,128)(2,1)S(1)} %get-tuple-element.23), channel_id=1, source_target_pairs={{0,2},{1,3},{2,0},{3,1},{4,6},{5,7},{6,4},{7,5},{8,10},{9,11},{10,... | collective-permute-start | bytes 245768 | tf_op jit(solution)/shard_map/ppermute | solution.py:30
  15.5 5.5 %collective-permute-done.2 = bf16[320,128]{1,0:T(8,128)(2,1)S(1)} collective-permute-done((bf16[320,128]{1,0:T(8,128)(2,1)S(1)}, bf16[320,128]{1,0:T(8,128)(2,1)S(1)}, u32[]{:S(2)}, u32[]{:S(2)}) %collective-permute-start.2) | collective-permute-done | bytes 81952 | tf_op jit(solution)/shard_map/ppermute | solution.py:30
  21.1 2.8 %shard_map.105 = bf16[1024,1280]{1,0:T(8,128)(2,1)S(1)} custom-call(bf16[1024,1280]{1,0:T(8,128)(2,1)} %collective-permute-done.first, bf16[1024,1280]{1,0:T(8,128)(2,1)S(1)} %bitcast.24, bf16[320,128]{1,0:T(8,128)(2,1)S(1)} %collective-permute-done.1.refs_0_, bf16[2,320,128]{2,1,0:T(8,128)(2,1)S(1)} %pad_maximum_fusion.refs_1_.refs_0_), custom_call_target="tpu_custom_call" | custom-call | tf_op jit(solution)/shard_map/pallas_call | solution.py:54
  23.8 2.2 collective-permute-start.4
  26.0 3.0 %collective-permute-start.5 = (bf16[2,320,128]{2,1,0:T(8,128)(2,1)S(1)}, bf16[2,320,128]{2,1,0:T(8,128)(2,1)S(1)}, u32[]{:S(2)}, u32[]{:S(2)}) collective-permute-start(bf16[2,320,128]{2,1,0:T(8,128)(2,1)S(1)} %pad_maximum_fusion.refs_1_.refs_0_), channel_id=1, source_target_pairs={{4,0},{8,4},{12,8},{0,12},{20,16},{24,20},{28,24},{16,28},{36,32},... | collective-permute-start | bytes 491528 | tf_op jit(solution)/shard_map/ppermute | solution.py:40
  29.0 2.8 %collective-permute-start.8 = (bf16[320,128]{1,0:T(8,128)(2,1)S(1)}, bf16[320,128]{1,0:T(8,128)(2,1)S(1)}, u32[]{:S(2)}, u32[]{:S(2)}) collective-permute-start(bf16[320,128]{1,0:T(8,128)(2,1)S(1)} %collective-permute-done.1.refs_0_), channel_id=1, source_target_pairs={{16,0},{20,4},{24,8},{28,12},{32,16},{36,20},{40,24},{44,28},{48,3... | collective-permute-start | bytes 245768 | tf_op jit(solution)/shard_map/ppermute | solution.py:35
  31.8 0.8 collective-permute-start.9
  32.6 0.9 collective-permute-start.10
  33.4 0.7 collective-permute-done.8.refs_1_
  34.8 3.7 %collective-permute-done.9.refs_2_ = bf16[320,128]{1,0:T(8,128)(2,1)S(1)} collective-permute-done((bf16[320,128]{1,0:T(8,128)(2,1)S(1)}, bf16[320,128]{1,0:T(8,128)(2,1)S(1)}, u32[]{:S(2)}, u32[]{:S(2)}) %collective-permute-start.9) | collective-permute-done | bytes 81952 | tf_op jit(solution)/shard_map/ppermute | solution.py:35
  38.5 1.8 collective-permute-done.10.refs_3_
  40.9 0.8 collective-permute-start.11
  42.1 1.0 collective-permute-start.13
  43.1 2.2 collective-permute-start.7
  45.2 18.0 %collective-permute-done.7.refs_3_ = bf16[2,320,128]{2,1,0:T(8,128)(2,1)S(1)} collective-permute-done((bf16[2,320,128]{2,1,0:T(8,128)(2,1)S(1)}, bf16[2,320,128]{2,1,0:T(8,128)(2,1)S(1)}, u32[]{:S(2)}, u32[]{:S(2)}) %collective-permute-start.7) | collective-permute-done | bytes 163872 | tf_op jit(solution)/shard_map/ppermute | solution.py:40
  63.8 0.8 copy-done.5
  65.6 0.7 copy-done.17
  66.3 0.8 collective-permute-start.14
  67.2 1.9 collective-permute-start.15
  69.1 1.0 collective-permute-start.17
  70.0 4.3 %fusion.1 = (f32[1024]{0:T(1024)S(1)}, bf16[1024,1280]{1,0:T(8,128)(2,1)S(1)}) fusion(bf16[1,1024,1280]{2,1,0:T(8,128)(2,1)S(1)} %copy-done.4, bf16[1024,1280]{1,0:T(8,128)(2,1)S(1)} %collective-permute-done.14, bf16[1024,1280]{1,0:T(8,128)(2,1)} %shard_map.108, bf16[1024,1280]{1,0:T(8,128)(2,1)} %collective-permute-done.first), kind=kLoop, calls=%fused_computation.3 | loop fusion | flops 17038336 | bytes 13111296 | tf_op jit(solution)/shard_map/reduce_sum | solution.py:407
  75.6 3.1 %shard_map.109 = (bf16[512,512]{1,0:T(8,128)(2,1)}, bf16[512,512]{1,0:T(8,128)(2,1)}) custom-call(s32[3]{0:T(128)S(1)} %pad_add_fusion.place.where, bf16[1024,1280]{1,0:T(8,128)(2,1)S(1)} %fusion.hs, bf16[1280,128]{1,0:T(8,128)(2,1)S(1)} %copy-done.8, bf16[1280,128]{1,0:T(8,128)(2,1)S(1)} %copy-done.14, bf16[1280,128]{1,0:T(8,128)(2,1)S(1)} %copy-done.16, ...), custom_call_target="tpu_custom_call" | custom-call | tf_op jit(solution)/shard_map/pallas_call | solution.py:337
  78.8 3.0 %collective-permute-start.18 = (bf16[512,512]{1,0:T(8,128)(2,1)}, bf16[512,512]{1,0:T(8,128)(2,1)}, u32[]{:S(2)}, u32[]{:S(2)}) collective-permute-start(bf16[512,512]{1,0:T(8,128)(2,1)} %get-tuple-element.26.after), channel_id=1, source_target_pairs={{0,1},{1,2},{2,3},{3,0},{4,5},{5,6},{6,7},{7,4},{8,9},{9,10},{10,1... | collective-permute-start | bytes 1572872 | tf_op jit(solution)/shard_map/ppermute | solution.py:30
  81.9 0.7 dynamic-slice_bitcast_fusion
  82.8 14.5 %collective-permute-done.15.refs_1_ = bf16[2,1280,128]{2,1,0:T(8,128)(2,1)} collective-permute-done((bf16[2,1280,128]{2,1,0:T(8,128)(2,1)S(1)}, bf16[2,1280,128]{2,1,0:T(8,128)(2,1)}, u32[]{:S(2)}, u32[]{:S(2)}) %collective-permute-start.15) | collective-permute-done | bytes 655392 | tf_op jit(solution)/shard_map/ppermute | solution.py:35
  97.3 3.5 %collective-permute-done.17.refs_3_ = bf16[2,1280,128]{2,1,0:T(8,128)(2,1)} collective-permute-done((bf16[2,1280,128]{2,1,0:T(8,128)(2,1)S(1)}, bf16[2,1280,128]{2,1,0:T(8,128)(2,1)}, u32[]{:S(2)}, u32[]{:S(2)}) %collective-permute-start.17) | collective-permute-done | bytes 655392 | tf_op jit(solution)/shard_map/ppermute | solution.py:35
  100.8 2.3 %shard_map.111.weight = bf16[1280,1024]{1,0:T(8,128)(2,1)S(1)} custom-call(s32[3]{0:T(128)S(1)} %pad_add_fusion.place.where, bf16[2,1280,128]{2,1,0:T(8,128)(2,1)S(1)} %copy-done.6, bf16[2,1280,128]{2,1,0:T(8,128)(2,1)} %collective-permute-done.15.refs_1_, bf16[2,1280,128]{2,1,0:T(8,128)(2,1)} %collective-permute-done.16.refs_2_, ...), custom_call_target="tpu_custom_call" | custom-call | tf_op jit(solution)/shard_map/pallas_call | solution.py:337
  103.1 2.5 %copy-done.3 = bf16[1,5120,512]{2,1,0:T(8,128)(2,1)S(1)} copy-done((bf16[1,5120,512]{2,1,0:T(8,128)(2,1)S(1)}, bf16[1,5120,512]{2,1,0:T(8,128)(2,1)}, u32[]{:S(2)}) %copy-start.3) | copy-done | bytes 5242904
  105.6 2.9 %shard_map.110 = (f32[1024,256]{1,0:T(8,128)S(1)}, f32[1024,128]{1,0:T(8,128)S(1)}, f32[1024,128]{1,0:T(8,128)S(1)}) custom-call(bf16[1024,1280]{1,0:T(8,128)(2,1)S(1)} %fusion.hs, bf16[5120,512]{1,0:T(8,128)(2,1)S(1)} %bitcast.22, s32[3]{0:T(128)S(1)} %pad_add_fusion.place.where, bf16[512,512]{1,0:T(8,128)(2,1)} %get-tuple-element.26.after), custom_call_target="tpu_custom_call" | custom-call | tf_op jit(solution)/shard_map/pallas_call | solution.py:337
  108.5 3.2 %shard_map.112 = (f32[128,128]{1,0:T(8,128)S(1)}, f32[128,128]{1,0:T(8,128)S(1)}, f32[128,128]{1,0:T(8,128)S(1)}) custom-call(s32[3]{0:T(128)S(1)} %pad_add_fusion.place.where, s32[4]{0:T(128)S(1)} %copy-done.30, bf16[16,1024]{1,0:T(8,128)(2,1)S(1)} %reshape_squeeze.6.queries, bf16[4,512,512]{2,1,0:T(8,128)(2,1)S(1)} %bitcast.25, ...), custom_call_target="tpu_custom_call" | custom-call | tf_op jit(solution)/shard_map/pallas_call | solution.py:337
  111.7 2.7 %shard_map.113 = (bf16[1024,256]{1,0:T(8,128)(2,1)S(1)}, bf16[1024,256]{1,0:T(8,128)(2,1)S(1)}) custom-call(bf16[1024,1280]{1,0:T(8,128)(2,1)S(1)} %fusion.hs, bf16[1280,1024]{1,0:T(8,128)(2,1)S(1)} %shard_map.111.weight, bf16[512,512]{1,0:T(8,128)(2,1)} %collective-permute-done.18.far_low, bf16[512,512]{1,0:T(8,128)(2,1)} %collective-permute-done.19.far_high, ...), custom_call_target="tpu_custom_call" | custom-call | tf_op jit(solution)/shard_map/pallas_call | solution.py:337
  114.4 2.5 %collective-permute-start.20 = (bf16[1024,256]{1,0:T(8,128)(2,1)S(1)}, bf16[1024,256]{1,0:T(8,128)(2,1)S(1)}, u32[]{:S(2)}, u32[]{:S(2)}) collective-permute-start(bf16[1024,256]{1,0:T(8,128)(2,1)S(1)} %get-tuple-element.32.refs_0_), channel_id=1, source_target_pairs={{0,1},{1,2},{2,3},{3,0},{4,5},{5,6},{6,7},{7,4},{8,9},{9,10},{10,1... | collective-permute-start | bytes 1572872 | tf_op jit(solution)/shard_map/ppermute | solution.py:30
  117.4 0.7 multiply_add_fusion
  118.2 1.9 collective-permute-start.24
  120.1 4.0 %collective-permute-start.23 = (f32[8,128]{1,0:T(8,128)S(1)}, f32[8,128]{1,0:T(8,128)S(1)}, u32[]{:S(2)}, u32[]{:S(2)}) collective-permute-start(f32[8,128]{1,0:T(8,128)S(1)} %bitcast.31), channel_id=1, source_target_pairs={{0,3},{1,0},{2,1},{3,2},{4,7},{5,4},{6,5},{7,6},{8,11},{9,8},{10,9... | collective-permute-start | bytes 12296 | tf_op jit(solution)/shard_map/ppermute | solution.py:30
  124.3 14.4 %collective-permute-done.24 = f32[8,128]{1,0:T(8,128)S(1)} collective-permute-done((f32[8,128]{1,0:T(8,128)S(1)}, f32[8,128]{1,0:T(8,128)S(1)}, u32[]{:S(2)}, u32[]{:S(2)}) %collective-permute-start.24) | collective-permute-done | bytes 4128 | tf_op jit(solution)/shard_map/ppermute | solution.py:30
  138.7 1.1 collective-permute-done.23
  140.0 2.4 %shard_map.114 = (bf16[1024,256]{1,0:T(8,128)(2,1)S(1)}, bf16[16,8,16,256]{3,2,1,0:T(8,128)(2,1)S(1)}) custom-call(s32[128]{0:T(128)S(1)} %select_reduce_fusion.source, f32[1024,256]{1,0:T(8,128)S(1)} %get-tuple-element.27.refs_3_.own, bf16[1024,256]{1,0:T(8,128)(2,1)S(1)} %collective-permute-done.20.ahead, ...), custom_call_target="tpu_custom_call" | custom-call | tf_op jit(solution)/shard_map/pallas_call | solution.py:337
  142.5 0.8 copy-done.9
  143.3 1.0 copy-done.19
  144.3 4.3 %all-to-all-start = ((bf16[16,8,16,256]{3,2,1,0:T(8,128)(2,1)}), bf16[16,8,16,256]{3,2,1,0:T(8,128)(2,1)}, u32[]{:S(2)}, u32[]{:S(2)}) async-start(bf16[16,8,16,256]{3,2,1,0:T(8,128)(2,1)} %copy-done.19), calls=%async_computation | async-start | bytes 2097152 | tf_op jit(solution)/shard_map/all_to_all | solution.py:491
  148.6 1.7 copy-done.1
  150.4 1.0 copy-done.25
  151.4 4.9 %shard_map.115 = (bf16[1024,128]{1,0:T(8,128)(2,1)}, bf16[1024,128]{1,0:T(8,128)(2,1)}, bf16[1024,128]{1,0:T(8,128)(2,1)S(1)}, bf16[1024,128]{1,0:T(8,128)(2,1)S(1)}) custom-call(bf16[1024,1280]{1,0:T(8,128)(2,1)S(1)} %fusion.hs, bf16[1280,1024]{1,0:T(8,128)(2,1)S(1)} %copy-done.1, bf16[512,512]{1,0:T(8,128)(2,1)} %collective-permute-done.18.far_low, ...), custom_call_target="tpu_custom_call" | custom-call | tf_op jit(solution)/shard_map/pallas_call | solution.py:337
  156.3 0.8 collective-permute-start.25
  157.0 2.2 collective-permute-start.26
  159.4 7.0 %collective-permute-done.25.ahead = bf16[1024,128]{1,0:T(8,128)(2,1)S(1)} collective-permute-done((bf16[1024,128]{1,0:T(8,128)(2,1)}, bf16[1024,128]{1,0:T(8,128)(2,1)S(1)}, u32[]{:S(2)}, u32[]{:S(2)}) %collective-permute-start.25) | collective-permute-done | bytes 262176 | tf_op jit(solution)/shard_map/ppermute | solution.py:30
  167.1 3.0 %collective-permute-done.26.behind = bf16[1024,128]{1,0:T(8,128)(2,1)S(1)} collective-permute-done((bf16[1024,128]{1,0:T(8,128)(2,1)}, bf16[1024,128]{1,0:T(8,128)(2,1)S(1)}, u32[]{:S(2)}, u32[]{:S(2)}) %collective-permute-start.26) | collective-permute-done | bytes 262176 | tf_op jit(solution)/shard_map/ppermute | solution.py:30
  170.8 1.0 copy-done.10
  171.9 1.0 copy-done.23
  172.9 0.9 copy-done.27
  173.9 0.9 copy-done.29
  174.8 4.2 %shard_map.116 = bf16[16,13,16,128]{3,2,1,0:T(8,128)(2,1)} custom-call(s32[3]{0:T(128)S(1)} %pad_add_fusion.place.where, s32[4]{0:T(128)S(1)} %bitcast.26, s32[128]{0:T(128)S(1)} %select_reduce_fusion.source, f32[1024,128]{1,0:T(8,128)S(1)} %copy-done.23, bf16[1024,128]{1,0:T(8,128)(2,1)S(1)} %copy-done.27, bf16[1024,128]{1,0:T(8,128)(2,1)S(1)} %copy-done.29, ...), custom_call_target="tpu_custom_call" | custom-call | tf_op jit(solution)/shard_map/pallas_call | solution.py:337
  179.0 6.8 %all-to-all-start.1 = ((bf16[16,13,16,128]{3,2,1,0:T(8,128)(2,1)}), bf16[16,13,16,128]{3,2,1,0:T(8,128)(2,1)S(1)}, u32[]{:S(2)}, u32[]{:S(2)}) async-start(bf16[16,13,16,128]{3,2,1,0:T(8,128)(2,1)} %shard_map.116), calls=%async_computation.1 | async-start | bytes 1703936 | tf_op jit(solution)/shard_map/all_to_all | solution.py:512
  186.3 2.5 %collective-permute-start.28 = (bf16[1024,128]{1,0:T(8,128)(2,1)}, bf16[1024,128]{1,0:T(8,128)(2,1)S(1)}, u32[]{:S(2)}, u32[]{:S(2)}) collective-permute-start(bf16[1024,128]{1,0:T(8,128)(2,1)} %copy-done.31), channel_id=1, source_target_pairs={{0,3},{1,0},{2,1},{3,2},{4,7},{5,4},{6,5},{7,6},{8,11},{9,8},{10,9... | collective-permute-start | bytes 786440 | tf_op jit(solution)/shard_map/ppermute | solution.py:30
  188.8 5.2 %collective-permute-done.27.ahead = bf16[1024,128]{1,0:T(8,128)(2,1)S(1)} collective-permute-done((bf16[1024,128]{1,0:T(8,128)(2,1)}, bf16[1024,128]{1,0:T(8,128)(2,1)S(1)}, u32[]{:S(2)}, u32[]{:S(2)}) %collective-permute-start.27) | collective-permute-done | bytes 262176 | tf_op jit(solution)/shard_map/ppermute | solution.py:30
  194.0 1.9 collective-permute-done.28.behind
  195.9 1.0 copy-done.21
  196.9 3.2 %shard_map.117 = bf16[16,13,16,128]{3,2,1,0:T(8,128)(2,1)S(1)} custom-call(s32[3]{0:T(128)S(1)} %pad_add_fusion.place.where, s32[4]{0:T(128)S(1)} %bitcast.27, s32[128]{0:T(128)S(1)} %select_reduce_fusion.source, f32[1024,128]{1,0:T(8,128)S(1)} %copy-done.21, bf16[1024,128]{1,0:T(8,128)(2,1)S(1)} %collective-permute-done.27.ahead, ...), custom_call_target="tpu_custom_call" | custom-call | tf_op jit(solution)/shard_map/pallas_call | solution.py:337
  200.2 19.1 %all_to_all.15.refs_2_ = bf16[16,13,16,128]{3,2,1,0:T(8,128)(2,1)S(1)} all-to-all(bf16[16,13,16,128]{3,2,1,0:T(8,128)(2,1)S(1)} %shard_map.117), channel_id=1, replica_groups=mesh['section'=4,'ctx'=16,'tp'=4] {'ctx'}, dimensions={0} | all-to-all | bytes 1703936 | tf_op jit(solution)/shard_map/all_to_all | solution.py:512
  219.3 3.3 %shard_map.118 = (bf16[128,16,512]{2,1,0:T(8,128)(2,1)}, bf16[16,1024]{1,0:T(8,128)(2,1)S(1)}) custom-call(bf16[16,8,16,256]{3,2,1,0:T(8,128)(2,1)} %all-to-all-done.refs_0_, bf16[16,13,16,128]{3,2,1,0:T(8,128)(2,1)S(1)} %all-to-all-done.1.refs_1_, bf16[16,13,16,128]{3,2,1,0:T(8,128)(2,1)S(1)} %all_to_all.15.refs_2_), custom_call_target="tpu_custom_call" | custom-call | tf_op jit(solution)/shard_map/pallas_call | solution.py:337
  (104 shorter events, 9.0 us)
Async XLA Ops:
  0.6 20.4 %collective-permute-start = (bf16[1024,1280]{1,0:T(8,128)(2,1)}, bf16[1024,1280]{1,0:T(8,128)(2,1)}, u32[]{:S(2)}, u32[]{:S(2)}) collective-permute-start(bf16[1024,1280]{1,0:T(8,128)(2,1)} %bitcast.23), channel_id=1, source_target_pairs={{0,64},{128,192},{1,65},{129,193},{2,66},{130,194},{3,67},{131,195... | collective-permute-start | bytes 7864328 | tf_op jit(solution)/shard_map/ppermute | solution.py:398
  3.9 2.5 %copy-start.2 = (bf16[1,5120,512]{2,1,0:T(8,128)(2,1)S(1)}, bf16[1,5120,512]{2,1,0:T(8,128)(2,1)}, u32[]{:S(2)}) copy-start(bf16[1,5120,512]{2,1,0:T(8,128)(2,1)} %param.11) | copy-start | bytes 15728644
  6.4 14.6 %copy-start.4 = (bf16[1,1024,1280]{2,1,0:T(8,128)(2,1)S(1)}, bf16[1,1024,1280]{2,1,0:T(8,128)(2,1)}, u32[]{:S(2)}) copy-start(bf16[1,1024,1280]{2,1,0:T(8,128)(2,1)} %param.9) | copy-start | bytes 7864324
  7.1 8.4 %collective-permute-start.3 = (bf16[320,128]{1,0:T(8,128)(2,1)S(1)}, bf16[320,128]{1,0:T(8,128)(2,1)S(1)}, u32[]{:S(2)}, u32[]{:S(2)}) collective-permute-start(bf16[320,128]{1,0:T(8,128)(2,1)S(1)} %get-tuple-element.25), channel_id=1, source_target_pairs={{0,1},{1,2},{2,3},{3,0},{4,5},{5,6},{6,7},{7,4},{8,9},{9,10},{10,1... | collective-permute-start | bytes 245768 | tf_op jit(solution)/shard_map/ppermute | solution.py:30
  11.6 9.4 %collective-permute-start.2 = (bf16[320,128]{1,0:T(8,128)(2,1)S(1)}, bf16[320,128]{1,0:T(8,128)(2,1)S(1)}, u32[]{:S(2)}, u32[]{:S(2)}) collective-permute-start(bf16[320,128]{1,0:T(8,128)(2,1)S(1)} %get-tuple-element.24), channel_id=1, source_target_pairs={{0,3},{1,0},{2,1},{3,2},{4,7},{5,4},{6,5},{7,6},{8,11},{9,8},{10,9... | collective-permute-start | bytes 245768 | tf_op jit(solution)/shard_map/ppermute | solution.py:30
  11.6 9.4 %collective-permute-start.1 = (bf16[320,128]{1,0:T(8,128)(2,1)S(1)}, bf16[320,128]{1,0:T(8,128)(2,1)S(1)}, u32[]{:S(2)}, u32[]{:S(2)}) collective-permute-start(bf16[320,128]{1,0:T(8,128)(2,1)S(1)} %get-tuple-element.23), channel_id=1, source_target_pairs={{0,2},{1,3},{2,0},{3,1},{4,6},{5,7},{6,4},{7,5},{8,10},{9,11},{10,... | collective-permute-start | bytes 245768 | tf_op jit(solution)/shard_map/ppermute | solution.py:30
  23.8 42.5 %collective-permute-start.4 = (bf16[1024,1280]{1,0:T(8,128)(2,1)S(1)}, bf16[1024,1280]{1,0:T(8,128)(2,1)}, u32[]{:S(2)}, u32[]{:S(2)}) collective-permute-start(bf16[1024,1280]{1,0:T(8,128)(2,1)S(1)} %shard_map.105), channel_id=1, source_target_pairs={{64,128},{65,129},{66,130},{67,131},{68,132},{69,133},{70,134},{71... | collective-permute-start | bytes 7864328 | tf_op jit(solution)/shard_map/ppermute | solution.py:399
  26.0 16.1 %collective-permute-start.5 = (bf16[2,320,128]{2,1,0:T(8,128)(2,1)S(1)}, bf16[2,320,128]{2,1,0:T(8,128)(2,1)S(1)}, u32[]{:S(2)}, u32[]{:S(2)}) collective-permute-start(bf16[2,320,128]{2,1,0:T(8,128)(2,1)S(1)} %pad_maximum_fusion.refs_1_.refs_0_), channel_id=1, source_target_pairs={{4,0},{8,4},{12,8},{0,12},{20,16},{24,20},{28,24},{16,28},{36,32},... | collective-permute-start | bytes 491528 | tf_op jit(solution)/shard_map/ppermute | solution.py:40
  29.0 5.2 %collective-permute-start.8 = (bf16[320,128]{1,0:T(8,128)(2,1)S(1)}, bf16[320,128]{1,0:T(8,128)(2,1)S(1)}, u32[]{:S(2)}, u32[]{:S(2)}) collective-permute-start(bf16[320,128]{1,0:T(8,128)(2,1)S(1)} %collective-permute-done.1.refs_0_), channel_id=1, source_target_pairs={{16,0},{20,4},{24,8},{28,12},{32,16},{36,20},{40,24},{44,28},{48,3... | collective-permute-start | bytes 245768 | tf_op jit(solution)/shard_map/ppermute | solution.py:35
  31.8 6.8 %collective-permute-start.9 = (bf16[320,128]{1,0:T(8,128)(2,1)S(1)}, bf16[320,128]{1,0:T(8,128)(2,1)S(1)}, u32[]{:S(2)}, u32[]{:S(2)}) collective-permute-start(bf16[320,128]{1,0:T(8,128)(2,1)S(1)} %collective-permute-done.1.refs_0_), channel_id=1, source_target_pairs={{32,0},{36,4},{40,8},{44,12},{48,16},{52,20},{56,24},{60,28},{0,32... | collective-permute-start | bytes 245768 | tf_op jit(solution)/shard_map/ppermute | solution.py:35
  32.6 7.8 %collective-permute-start.10 = (bf16[320,128]{1,0:T(8,128)(2,1)S(1)}, bf16[320,128]{1,0:T(8,128)(2,1)S(1)}, u32[]{:S(2)}, u32[]{:S(2)}) collective-permute-start(bf16[320,128]{1,0:T(8,128)(2,1)S(1)} %collective-permute-done.1.refs_0_), channel_id=1, source_target_pairs={{48,0},{52,4},{56,8},{60,12},{0,16},{4,20},{8,24},{12,28},{16,32},... | collective-permute-start | bytes 245768 | tf_op jit(solution)/shard_map/ppermute | solution.py:35
  34.2 8.9 %collective-permute-start.6 = (bf16[2,320,128]{2,1,0:T(8,128)(2,1)S(1)}, bf16[2,320,128]{2,1,0:T(8,128)(2,1)S(1)}, u32[]{:S(2)}, u32[]{:S(2)}) collective-permute-start(bf16[2,320,128]{2,1,0:T(8,128)(2,1)S(1)} %pad_maximum_fusion.refs_1_.refs_0_), channel_id=1, source_target_pairs={{8,0},{12,4},{0,8},{4,12},{24,16},{28,20},{16,24},{20,28},{40,32},... | collective-permute-start | bytes 491528 | tf_op jit(solution)/shard_map/ppermute | solution.py:40
  40.9 22.9 %copy-start.7 = (bf16[1280,128]{1,0:T(8,128)(2,1)}, bf16[1280,128]{1,0:T(8,128)(2,1)S(1)}, u32[]{:S(2)}) copy-start(bf16[1280,128]{1,0:T(8,128)(2,1)S(1)} %shard_map.107.refs_2_.refs_0_) | copy-start | bytes 983044
  40.9 23.8 %collective-permute-start.11 = (bf16[1280,128]{1,0:T(8,128)(2,1)S(1)}, bf16[1280,128]{1,0:T(8,128)(2,1)S(1)}, u32[]{:S(2)}, u32[]{:S(2)}) collective-permute-start(bf16[1280,128]{1,0:T(8,128)(2,1)S(1)} %shard_map.107.refs_2_.refs_0_), channel_id=1, source_target_pairs={{4,0},{8,4},{12,8},{0,12},{20,16},{24,20},{28,24},{16,28},{36,32},... | collective-permute-start | bytes 983048 | tf_op jit(solution)/shard_map/ppermute | solution.py:40
  41.7 22.9 %collective-permute-start.12 = (bf16[1280,128]{1,0:T(8,128)(2,1)S(1)}, bf16[1280,128]{1,0:T(8,128)(2,1)S(1)}, u32[]{:S(2)}, u32[]{:S(2)}) collective-permute-start(bf16[1280,128]{1,0:T(8,128)(2,1)S(1)} %shard_map.107.refs_2_.refs_0_), channel_id=1, source_target_pairs={{8,0},{12,4},{0,8},{4,12},{24,16},{28,20},{16,24},{20,28},{40,32},... | collective-permute-start | bytes 983048 | tf_op jit(solution)/shard_map/ppermute | solution.py:40
  42.1 22.6 %collective-permute-start.13 = (bf16[1280,128]{1,0:T(8,128)(2,1)S(1)}, bf16[1280,128]{1,0:T(8,128)(2,1)S(1)}, u32[]{:S(2)}, u32[]{:S(2)}) collective-permute-start(bf16[1280,128]{1,0:T(8,128)(2,1)S(1)} %shard_map.107.refs_2_.refs_0_), channel_id=1, source_target_pairs={{12,0},{0,4},{4,8},{8,12},{28,16},{16,20},{20,24},{24,28},{44,32},... | collective-permute-start | bytes 983048 | tf_op jit(solution)/shard_map/ppermute | solution.py:40
  43.1 20.2 %collective-permute-start.7 = (bf16[2,320,128]{2,1,0:T(8,128)(2,1)S(1)}, bf16[2,320,128]{2,1,0:T(8,128)(2,1)S(1)}, u32[]{:S(2)}, u32[]{:S(2)}) collective-permute-start(bf16[2,320,128]{2,1,0:T(8,128)(2,1)S(1)} %pad_maximum_fusion.refs_1_.refs_0_), channel_id=1, source_target_pairs={{12,0},{0,4},{4,8},{8,12},{28,16},{16,20},{20,24},{24,28},{44,32},... | collective-permute-start | bytes 491528 | tf_op jit(solution)/shard_map/ppermute | solution.py:40
  63.8 0.8 copy-start.5
  64.7 2.5 %copy-start.35 = (bf16[1,1280]{1,0:T(2,128)(2,1)S(1)}, bf16[1,1280]{1,0:T(2,128)(2,1)}, u32[]{:S(2)}) copy-start(bf16[1,1280]{1,0:T(2,128)(2,1)} %param.10) | copy-start | bytes 7684
  64.7 2.5 %copy-start.6 = (bf16[2,1280,128]{2,1,0:T(8,128)(2,1)S(1)}, bf16[2,1280,128]{2,1,0:T(8,128)(2,1)}, u32[]{:S(2)}) copy-start(bf16[2,1280,128]{2,1,0:T(8,128)(2,1)} %copy-done.5) | copy-start | bytes 1966084
  64.7 0.9 copy-start.15
  66.3 3.7 %collective-permute-start.14 = (bf16[1024,1280]{1,0:T(8,128)(2,1)}, bf16[1024,1280]{1,0:T(8,128)(2,1)S(1)}, u32[]{:S(2)}, u32[]{:S(2)}) collective-permute-start(bf16[1024,1280]{1,0:T(8,128)(2,1)} %shard_map.108), channel_id=1, source_target_pairs={{128,192},{129,193},{130,194},{131,195},{132,196},{133,197},{134,1... | collective-permute-start | bytes 7864328 | tf_op jit(solution)/shard_map/ppermute | solution.py:401
  67.2 30.1 %collective-permute-start.15 = (bf16[2,1280,128]{2,1,0:T(8,128)(2,1)S(1)}, bf16[2,1280,128]{2,1,0:T(8,128)(2,1)}, u32[]{:S(2)}, u32[]{:S(2)}) collective-permute-start(bf16[2,1280,128]{2,1,0:T(8,128)(2,1)S(1)} %copy-done.6), channel_id=1, source_target_pairs={{16,0},{20,4},{24,8},{28,12},{32,16},{36,20},{40,24},{44,28},{48,3... | collective-permute-start | bytes 1966088 | tf_op jit(solution)/shard_map/ppermute | solution.py:35
  69.1 28.3 %collective-permute-start.16 = (bf16[2,1280,128]{2,1,0:T(8,128)(2,1)S(1)}, bf16[2,1280,128]{2,1,0:T(8,128)(2,1)}, u32[]{:S(2)}, u32[]{:S(2)}) collective-permute-start(bf16[2,1280,128]{2,1,0:T(8,128)(2,1)S(1)} %copy-done.6), channel_id=1, source_target_pairs={{32,0},{36,4},{40,8},{44,12},{48,16},{52,20},{56,24},{60,28},{0,32... | collective-permute-start | bytes 1966088 | tf_op jit(solution)/shard_map/ppermute | solution.py:35
  69.1 31.7 %collective-permute-start.17 = (bf16[2,1280,128]{2,1,0:T(8,128)(2,1)S(1)}, bf16[2,1280,128]{2,1,0:T(8,128)(2,1)}, u32[]{:S(2)}, u32[]{:S(2)}) collective-permute-start(bf16[2,1280,128]{2,1,0:T(8,128)(2,1)S(1)} %copy-done.6), channel_id=1, source_target_pairs={{48,0},{52,4},{56,8},{60,12},{0,16},{4,20},{8,24},{12,28},{16,32},... | collective-permute-start | bytes 1966088 | tf_op jit(solution)/shard_map/ppermute | solution.py:35
  74.4 1.0 copy-start.8
  74.4 1.1 copy-start.14
  74.4 1.2 copy-start.16
  74.4 1.2 copy-start.18
  75.6 6.2 %copy-start.33 = (bf16[1,4,4,1024]{3,2,1,0:T(4,128)(2,1)S(1)}, bf16[1,4,4,1024]{3,2,1,0:T(4,128)(2,1)}, u32[]{:S(2)}) copy-start(bf16[1,4,4,1024]{3,2,1,0:T(4,128)(2,1)} %param.16) | copy-start | bytes 98308
  75.6 6.2 %copy-start.34 = (bf16[1,4,4,512]{3,2,1,0:T(4,128)(2,1)S(1)}, bf16[1,4,4,512]{3,2,1,0:T(4,128)(2,1)}, u32[]{:S(2)}) copy-start(bf16[1,4,4,512]{3,2,1,0:T(4,128)(2,1)} %param.17) | copy-start | bytes 49156
  78.8 32.9 %collective-permute-start.18 = (bf16[512,512]{1,0:T(8,128)(2,1)}, bf16[512,512]{1,0:T(8,128)(2,1)}, u32[]{:S(2)}, u32[]{:S(2)}) collective-permute-start(bf16[512,512]{1,0:T(8,128)(2,1)} %get-tuple-element.26.after), channel_id=1, source_target_pairs={{0,1},{1,2},{2,3},{3,0},{4,5},{5,6},{6,7},{7,4},{8,9},{9,10},{10,1... | collective-permute-start | bytes 1572872 | tf_op jit(solution)/shard_map/ppermute | solution.py:30
  81.8 29.8 %collective-permute-start.19 = (bf16[512,512]{1,0:T(8,128)(2,1)}, bf16[512,512]{1,0:T(8,128)(2,1)}, u32[]{:S(2)}, u32[]{:S(2)}) collective-permute-start(bf16[512,512]{1,0:T(8,128)(2,1)} %get-tuple-element.28), channel_id=1, source_target_pairs={{0,3},{1,0},{2,1},{3,2},{4,7},{5,4},{6,5},{7,6},{8,11},{9,8},{10,9... | collective-permute-start | bytes 1572872 | tf_op jit(solution)/shard_map/ppermute | solution.py:30
  103.1 2.5 %copy-start.3 = (bf16[1,5120,512]{2,1,0:T(8,128)(2,1)S(1)}, bf16[1,5120,512]{2,1,0:T(8,128)(2,1)}, u32[]{:S(2)}) copy-start(bf16[1,5120,512]{2,1,0:T(8,128)(2,1)} %param.11) | copy-start | bytes 15728644
  105.6 6.1 %copy-start = (bf16[1280,1024]{1,0:T(8,128)(2,1)}, bf16[1280,1024]{1,0:T(8,128)(2,1)S(1)}, u32[]{:S(2)}) copy-start(bf16[1280,1024]{1,0:T(8,128)(2,1)S(1)} %shard_map.111.weight) | copy-start | bytes 7864324
  105.6 2.9 %copy-start.12 = (bf16[1,4,512,512]{3,2,1,0:T(8,128)(2,1)S(1)}, bf16[1,4,512,512]{3,2,1,0:T(8,128)(2,1)}, u32[]{:S(2)}) copy-start(bf16[1,4,512,512]{3,2,1,0:T(8,128)(2,1)} %param.15) | copy-start | bytes 6291460
  105.6 2.9 %copy-start.30 = (s32[4]{0:T(128)S(1)}, s32[4]{0:T(128)}, u32[]{:S(2)}) copy-start(s32[4]{0:T(128)} %lengths.1) | copy-start | bytes 52
  108.4 6.0 %copy-start.20 = (f32[1024,128]{1,0:T(8,128)}, f32[1024,128]{1,0:T(8,128)S(1)}, u32[]{:S(2)}) copy-start(f32[1024,128]{1,0:T(8,128)S(1)} %get-tuple-element.39.own) | copy-start | bytes 1572868
  108.4 6.0 %copy-start.22 = (f32[1024,128]{1,0:T(8,128)}, f32[1024,128]{1,0:T(8,128)S(1)}, u32[]{:S(2)}) copy-start(f32[1024,128]{1,0:T(8,128)S(1)} %get-tuple-element.35.own) | copy-start | bytes 1572868
  114.4 28.1 %copy-start.24 = (bf16[1024,256]{1,0:T(8,128)(2,1)}, bf16[1024,256]{1,0:T(8,128)(2,1)S(1)}, u32[]{:S(2)}) copy-start(bf16[1024,256]{1,0:T(8,128)(2,1)S(1)} %get-tuple-element.32.refs_0_) | copy-start | bytes 1572868
  114.4 25.4 %collective-permute-start.20 = (bf16[1024,256]{1,0:T(8,128)(2,1)S(1)}, bf16[1024,256]{1,0:T(8,128)(2,1)S(1)}, u32[]{:S(2)}, u32[]{:S(2)}) collective-permute-start(bf16[1024,256]{1,0:T(8,128)(2,1)S(1)} %get-tuple-element.32.refs_0_), channel_id=1, source_target_pairs={{0,1},{1,2},{2,3},{3,0},{4,5},{5,6},{6,7},{7,4},{8,9},{9,10},{10,1... | collective-permute-start | bytes 1572872 | tf_op jit(solution)/shard_map/ppermute | solution.py:30
  116.9 22.9 %collective-permute-start.21 = (bf16[1024,256]{1,0:T(8,128)(2,1)S(1)}, bf16[1024,256]{1,0:T(8,128)(2,1)S(1)}, u32[]{:S(2)}, u32[]{:S(2)}) collective-permute-start(bf16[1024,256]{1,0:T(8,128)(2,1)S(1)} %get-tuple-element.33), channel_id=1, source_target_pairs={{0,3},{1,0},{2,1},{3,2},{4,7},{5,4},{6,5},{7,6},{8,11},{9,8},{10,9... | collective-permute-start | bytes 1572872 | tf_op jit(solution)/shard_map/ppermute | solution.py:30
  118.2 20.5 %collective-permute-start.24 = (f32[8,128]{1,0:T(8,128)S(1)}, f32[8,128]{1,0:T(8,128)S(1)}, u32[]{:S(2)}, u32[]{:S(2)}) collective-permute-start(f32[8,128]{1,0:T(8,128)S(1)} %bitcast.30), channel_id=1, source_target_pairs={{0,2},{1,3},{2,0},{3,1},{4,6},{5,7},{6,4},{7,5},{8,10},{9,11},{10,... | collective-permute-start | bytes 12296 | tf_op jit(solution)/shard_map/ppermute | solution.py:30
  120.1 19.7 %collective-permute-start.23 = (f32[8,128]{1,0:T(8,128)S(1)}, f32[8,128]{1,0:T(8,128)S(1)}, u32[]{:S(2)}, u32[]{:S(2)}) collective-permute-start(f32[8,128]{1,0:T(8,128)S(1)} %bitcast.31), channel_id=1, source_target_pairs={{0,3},{1,0},{2,1},{3,2},{4,7},{5,4},{6,5},{7,6},{8,11},{9,8},{10,9... | collective-permute-start | bytes 12296 | tf_op jit(solution)/shard_map/ppermute | solution.py:30
  124.1 15.7 %collective-permute-start.22 = (f32[8,128]{1,0:T(8,128)S(1)}, f32[8,128]{1,0:T(8,128)S(1)}, u32[]{:S(2)}, u32[]{:S(2)}) collective-permute-start(f32[8,128]{1,0:T(8,128)S(1)} %bitcast.32), channel_id=1, source_target_pairs={{0,1},{1,2},{2,3},{3,0},{4,5},{5,6},{6,7},{7,4},{8,9},{9,10},{10,1... | collective-permute-start | bytes 12296 | tf_op jit(solution)/shard_map/ppermute | solution.py:30
  142.5 0.8 copy-start.9
  143.3 1.0 copy-start.19
  144.3 34.7 %all-to-all-start = ((bf16[16,8,16,256]{3,2,1,0:T(8,128)(2,1)}), bf16[16,8,16,256]{3,2,1,0:T(8,128)(2,1)}, u32[]{:S(2)}, u32[]{:S(2)}) async-start(bf16[16,8,16,256]{3,2,1,0:T(8,128)(2,1)} %copy-done.19), calls=%async_computation | async-start | bytes 2097152 | tf_op jit(solution)/shard_map/all_to_all | solution.py:491
  148.6 1.7 copy-start.1
  150.4 1.0 copy-start.25
  151.4 7.8 %copy-start.36 = (s32[4]{0:T(128)S(1)}, s32[4]{0:T(128)}, u32[]{:S(2)}) copy-start(s32[4]{0:T(128)} %param.12) | copy-start | bytes 52
  156.3 2.9 %copy-start.31 = (bf16[1024,128]{1,0:T(8,128)(2,1)}, bf16[1024,128]{1,0:T(8,128)(2,1)S(1)}, u32[]{:S(2)}) copy-start(bf16[1024,128]{1,0:T(8,128)(2,1)S(1)} %get-tuple-element.41) | copy-start | bytes 786436
  156.3 2.9 %copy-start.32 = (bf16[1024,128]{1,0:T(8,128)(2,1)}, bf16[1024,128]{1,0:T(8,128)(2,1)S(1)}, u32[]{:S(2)}) copy-start(bf16[1024,128]{1,0:T(8,128)(2,1)S(1)} %get-tuple-element.40) | copy-start | bytes 786436
  156.3 10.1 %collective-permute-start.25 = (bf16[1024,128]{1,0:T(8,128)(2,1)}, bf16[1024,128]{1,0:T(8,128)(2,1)S(1)}, u32[]{:S(2)}, u32[]{:S(2)}) collective-permute-start(bf16[1024,128]{1,0:T(8,128)(2,1)} %get-tuple-element.36), channel_id=1, source_target_pairs={{0,1},{1,2},{2,3},{3,0},{4,5},{5,6},{6,7},{7,4},{8,9},{9,10},{10,1... | collective-permute-start | bytes 786440 | tf_op jit(solution)/shard_map/ppermute | solution.py:30
  157.0 13.1 %collective-permute-start.26 = (bf16[1024,128]{1,0:T(8,128)(2,1)}, bf16[1024,128]{1,0:T(8,128)(2,1)S(1)}, u32[]{:S(2)}, u32[]{:S(2)}) collective-permute-start(bf16[1024,128]{1,0:T(8,128)(2,1)} %get-tuple-element.37), channel_id=1, source_target_pairs={{0,3},{1,0},{2,1},{3,2},{4,7},{5,4},{6,5},{7,6},{8,11},{9,8},{10,9... | collective-permute-start | bytes 786440 | tf_op jit(solution)/shard_map/ppermute | solution.py:30
  170.8 1.0 copy-start.10
  171.9 1.0 copy-start.23
  172.9 0.9 copy-start.27
  173.9 0.9 copy-start.29
  174.8 21.1 %copy-start.11 = (bf16[1024,256]{1,0:T(8,128)(2,1)S(1)}, bf16[1024,256]{1,0:T(8,128)(2,1)}, u32[]{:S(2)}) copy-start(bf16[1024,256]{1,0:T(8,128)(2,1)} %copy-done.9) | copy-start | bytes 1572868
  179.0 21.2 %all-to-all-start.1 = ((bf16[16,13,16,128]{3,2,1,0:T(8,128)(2,1)}), bf16[16,13,16,128]{3,2,1,0:T(8,128)(2,1)S(1)}, u32[]{:S(2)}, u32[]{:S(2)}) async-start(bf16[16,13,16,128]{3,2,1,0:T(8,128)(2,1)} %shard_map.116), calls=%async_computation.1 | async-start | bytes 1703936 | tf_op jit(solution)/shard_map/all_to_all | solution.py:512
  185.8 8.2 %collective-permute-start.27 = (bf16[1024,128]{1,0:T(8,128)(2,1)}, bf16[1024,128]{1,0:T(8,128)(2,1)S(1)}, u32[]{:S(2)}, u32[]{:S(2)}) collective-permute-start(bf16[1024,128]{1,0:T(8,128)(2,1)} %copy-done.32), channel_id=1, source_target_pairs={{0,1},{1,2},{2,3},{3,0},{4,5},{5,6},{6,7},{7,4},{8,9},{9,10},{10,1... | collective-permute-start | bytes 786440 | tf_op jit(solution)/shard_map/ppermute | solution.py:30
  186.3 9.6 %collective-permute-start.28 = (bf16[1024,128]{1,0:T(8,128)(2,1)}, bf16[1024,128]{1,0:T(8,128)(2,1)S(1)}, u32[]{:S(2)}, u32[]{:S(2)}) collective-permute-start(bf16[1024,128]{1,0:T(8,128)(2,1)} %copy-done.31), channel_id=1, source_target_pairs={{0,3},{1,0},{2,1},{3,2},{4,7},{5,4},{6,5},{7,6},{8,11},{9,8},{10,9... | collective-permute-start | bytes 786440 | tf_op jit(solution)/shard_map/ppermute | solution.py:30
  195.9 1.0 copy-start.21
  (4 other events, 2.9 us)

commit v2 on v1

v2 whole, which is shorter than its diff:
```python
import functools

import jax
import jax.numpy as jnp
from jax import lax
from jax.experimental import pallas as pl
from jax.experimental.pallas import tpu as pltpu
from jax.sharding import PartitionSpec as P

D = 5120
HEAD_DIM = 128
SESSIONS = 4
STEPS = 4
PAGE = 16
SIDE = 4

epsilon = 1e-05
floor_value = -1e30
bf16 = jnp.bfloat16
f32 = jnp.float32
TOKEN = jax.ShapeDtypeStruct((8, HEAD_DIM), jnp.float32)
VMEM = pl.BlockSpec(memory_space=pltpu.VMEM)
SMEM = pl.BlockSpec(memory_space=pltpu.SMEM)
ANY = pl.BlockSpec(memory_space=pl.ANY)
HBM = pl.BlockSpec(memory_space=pltpu.HBM)
MEBI = 1024 * 1024
SOME_COST = pl.CostEstimate(flops=8_000_000_000, bytes_accessed=0, transcendentals=0)
NO_COST = pl.CostEstimate(flops=0, bytes_accessed=0, transcendentals=0)


def shift_tp(array, by):
    peers = lax.axis_size("tp")
    return lax.ppermute(array, "tp", [(i, (i + by) % peers) for i in range(peers)])


def from_x(array, by):
    pairs = [(((i // SIDE + by) % SIDE) * SIDE + i % SIDE, i) for i in range(SIDE * SIDE)]
    return lax.ppermute(array, "ctx", pairs)


def from_y(array, by):
    pairs = [((i // SIDE) * SIDE + (i % SIDE + by) % SIDE, i) for i in range(SIDE * SIDE)]
    return lax.ppermute(array, "ctx", pairs)


def added(first, second):
    return (first.astype(f32) + second.astype(f32)).astype(bf16)


def add_kernel(first, second, *refs):
    refs[-1][...] = added(first[...], second[...])


def add_after(first, second, *after):
    rows, columns = first.shape
    block = pl.BlockSpec((rows // 4, columns), lambda i: (i, 0))
    return pl.pallas_call(
        add_kernel,
        grid=(4,),
        out_shape=jax.ShapeDtypeStruct(first.shape, bf16),
        in_specs=[block, block] + [VMEM] * len(after),
        out_specs=block,
        compiler_params=pltpu.CompilerParams(vmem_limit_bytes=8 * MEBI),
        cost_estimate=SOME_COST,
    )(first, second, *after)


def token_kernel(*refs):
    refs[-1][...] = jnp.zeros(refs[-1].shape, refs[-1].dtype)


def nothing(*refs):
    pass


def tied(array, *after):
    return pl.pallas_call(
        nothing,
        out_shape=jax.ShapeDtypeStruct(array.shape, array.dtype),
        in_specs=[VMEM] * (1 + len(after)),
        out_specs=VMEM,
        input_output_aliases={0: 0},
        compiler_params=pltpu.CompilerParams(vmem_limit_bytes=8 * MEBI),
        cost_estimate=NO_COST,
    )(array, *after)


def tied_pair(first, second, *after):
    shapes = [jax.ShapeDtypeStruct(a.shape, a.dtype) for a in (first, second)]
    return pl.pallas_call(
        nothing,
        out_shape=shapes,
        in_specs=[VMEM] * (2 + len(after)),
        out_specs=[VMEM, VMEM],
        input_output_aliases={0: 0, 1: 1},
        compiler_params=pltpu.CompilerParams(vmem_limit_bytes=8 * MEBI),
        cost_estimate=NO_COST,
    )(first, second, *after)


def pieces_kernel(place, weight, one, three, far, sems):
    x, y, rank = place[0], place[1], place[2]
    rows = one.shape[0]
    features = rows * SIDE
    copies = []
    for n, (out, behind, row, column) in enumerate(((one, 1, y, x), (three, 3, y, x), (far, 2, x, y))):
        start = lax.rem(rank + SIDE - behind, SIDE) * features + row * rows
        copies.append(
            pltpu.make_async_copy(
                weight.at[
                    pl.ds(pl.multiple_of(start, rows), rows),
                    pl.ds(pl.multiple_of(column * HEAD_DIM, HEAD_DIM), HEAD_DIM),
                ],
                out,
                sems.at[n],
            )
        )
    for copy in copies:
        copy.start()
    for copy in copies:
        copy.wait()


def rows_kernel(axis, place, *refs):
    out, token = refs[-2:]
    rows = refs[0].shape[-2]
    for k in range(SIDE):
        start = pl.multiple_of(lax.rem(place[axis] + k, SIDE) * rows, rows)
        if len(out.shape) == 2:
            out[pl.ds(start, rows), :] = refs[k][...]
        else:
            out[:, pl.ds(start, rows), :] = refs[k][...]
    token[...] = jnp.zeros(token.shape, token.dtype)


def columns_kernel(place, *refs):
    out = refs[-1]
    half = out.shape[1] // 2
    for k in range(SIDE):
        start = lax.rem(place[0] + k, SIDE) * HEAD_DIM
        for n in range(2):
            out[:, pl.ds(pl.multiple_of(n * half + start, HEAD_DIM), HEAD_DIM)] = refs[k][n]


def dot_rows(hs, weight, start):
    return jnp.dot(hs[start : start + 256, :], weight, preferred_element_type=f32)


def to_terms(sums, width):
    high = sums.astype(bf16).astype(f32)
    middle = (sums - high).astype(bf16).astype(f32)
    low = sums - high - middle
    blank = jnp.zeros(sums.shape, f32)
    pad = [jnp.zeros((16, width - 2 * HEAD_DIM), f32)] if width > 2 * HEAD_DIM else []
    first = jnp.concatenate([high, low], axis=0)
    second = jnp.concatenate([middle, blank], axis=0)
    return jnp.concatenate([first, second] + pad, axis=1).astype(bf16)


def from_terms(rows):
    rows = rows.astype(f32)
    return rows[:8, :HEAD_DIM] + rows[:8, HEAD_DIM : 2 * HEAD_DIM] + rows[8:, :HEAD_DIM]


def far_kernel(where, squares, hs, *refs):
    parts, (low, high, token), held, sems = refs[:SIDE], refs[SIDE : SIDE + 3], refs[-2], refs[-1]
    token[...] = jnp.zeros(token.shape, token.dtype)
    copies = []
    for k in range(SIDE):
        column = pl.multiple_of(lax.rem(where[1] + k, SIDE) * HEAD_DIM, HEAD_DIM)
        copies.append(pltpu.make_async_copy(parts[k], held.at[:, pl.ds(column, HEAD_DIM)], sems.at[k]))
    for copy in copies:
        copy.start()
    for copy in copies:
        copy.wait()
    cut = hs.shape[0] - high.shape[0]
    for start in range(0, hs.shape[0], 256):
        out, at = (low, start) if start < cut else (high, start - cut)
        out[at : at + 256, :] = dot_rows(hs, held[...], start).astype(bf16)
    low[cut:, :] = to_terms(squares[...], low.shape[1])


def hidden_kernel(info, chip, crossed, passed, gain, hs, squares):
    step = pl.program_id(0)
    groups = hs.shape[0] // HEAD_DIM

    @pl.when(step == 0)
    def _():
        squares[...] = jnp.zeros(squares.shape, f32)

    wide = chip[...].astype(f32) + crossed[...].astype(f32) + passed[...].astype(f32)
    wide = wide.astype(bf16).astype(f32)
    hs[...] = (wide * gain[...].astype(f32)).astype(bf16)
    sums = jnp.sum(wide * wide, axis=1, keepdims=True)
    line = lax.broadcasted_iota(jnp.int32, squares.shape, 0)
    for n in range(groups):
        turned = jnp.broadcast_to(sums[n * HEAD_DIM : (n + 1) * HEAD_DIM], (HEAD_DIM, HEAD_DIM)).T[:8]
        squares[...] = jnp.where(line == step * groups + n, turned, squares[...])


def hidden_state(info, chip, crossed, passed, gain):
    rows, features = chip.shape
    block = rows // 4

    def wanted(*sections):
        def index(i, info):
            needed = functools.reduce(jnp.logical_or, [info[3] == s for s in sections])
            return jnp.where(needed, i, 0), 0

        return pl.BlockSpec((block, features), index)

    return pl.pallas_call(
        hidden_kernel,
        grid_spec=pltpu.PrefetchScalarGridSpec(
            num_scalar_prefetch=1,
            grid=(4,),
            in_specs=[
                wanted(0, 1, 2, 3),
                wanted(2),
                wanted(3),
                pl.BlockSpec((1, features), lambda i, info: (0, 0)),
            ],
            out_specs=[
                pl.BlockSpec((block, features), lambda i, info: (i, 0)),
                pl.BlockSpec((8, HEAD_DIM), lambda i, info: (0, 0)),
            ],
        ),
        out_shape=[jax.ShapeDtypeStruct((rows, features), bf16), TOKEN],
        compiler_params=pltpu.CompilerParams(vmem_limit_bytes=16 * MEBI),
        cost_estimate=SOME_COST,
    )(info, chip, crossed, passed, gain)


def own_kernel(hs, weight, place, after, *refs):
    outs, token, held, sem = refs[:-3], refs[-3], refs[-2], refs[-1]
    token[...] = jnp.zeros(token.shape, token.dtype)
    rows = held.shape[0]
    copy = pltpu.make_async_copy(weight.at[pl.ds(pl.multiple_of(place[2] * rows, rows), rows)], held, sem)
    copy.start()
    copy.wait()
    for start in range(0, hs.shape[0], 256):
        column = 0
        for out in outs:
            width = out.shape[1]
            out[start : start + 256, :] = dot_rows(hs, held[:, column : column + width], start)
            column += width


def near_kernel(widths, squares, hs, weight, far_low, far_high, *refs):
    outs, token = refs[:-1], refs[-1]
    token[...] = jnp.zeros(token.shape, token.dtype)
    rows = hs.shape[0]
    columns = far_low.shape[1]
    cut = rows - far_high.shape[0]
    column = 0
    for n, width in enumerate(widths):
        cols = slice(column, column + width)
        for start in range(0, rows, 256):
            block = slice(start, start + 256)
            ahead = dot_rows(hs, weight[:, cols], start)
            behind = dot_rows(hs, weight[:, columns + column : columns + column + width], start)
            if start < cut:
                ahead = ahead + far_low[block, cols].astype(f32)
            else:
                behind = behind + far_high[start - cut : start - cut + 256, cols].astype(f32)
            outs[2 * n][block, :] = ahead.astype(bf16)
            outs[2 * n + 1][block, :] = behind.astype(bf16)
        column += width
    width = widths[0]
    outs[0][rows:, :] = to_terms(squares[...] + from_terms(far_low[cut:, :]), width)
    outs[1][rows:, :] = to_terms(squares[...], width)


def lay_pages(source, fresh, payload):
    owners, capacity = payload.shape[0], source.shape[0] // payload.shape[0]

    def place(owner, carry):
        for r in range(capacity):
            page = source[owner * capacity + r]
            payload[owner, r] = fresh[pl.ds(pl.multiple_of(page * PAGE, PAGE), PAGE), :]
        return carry

    lax.fori_loop(0, owners, place, 0)


def sum_rows(own, ahead, behind, scale, fresh):
    for n in range(own.shape[0] // HEAD_DIM):
        block = slice(n * HEAD_DIM, (n + 1) * HEAD_DIM)
        factor = jnp.broadcast_to(scale[n : n + 1, :], (HEAD_DIM, HEAD_DIM)).T[:, :1]
        total = own[block, :] + ahead[block, :].astype(f32) + behind[block, :].astype(f32)
        fresh[block, :] = (total * factor).astype(bf16)
    fresh[own.shape[0] :, :] = jnp.zeros((PAGE, fresh.shape[1]), bf16)


def keys_kernel(
    heads, place, ends, source, squares, own, ahead, behind, queries, peak, total, mixed, *refs
):
    scale, fresh, payload, weights_out, level_out, mixed_out = refs
    rows = own.shape[0]
    sums = squares[...] + from_terms(ahead[rows:, :]) + from_terms(behind[rows:, :])
    scale[...] = lax.rsqrt(sums / D + epsilon)
    sum_rows(own, ahead, behind, scale, fresh)
    lay_pages(source, fresh, payload)
    lines = peak.shape[0] // heads
    group = lines // (SESSIONS * STEPS)
    ctx = place[0] * SIDE + place[1]
    session, step, key = row_ids(lines, rows)
    page = key // PAGE + ctx * (rows // PAGE)
    owner_session = jnp.zeros_like(page)
    for s in range(SESSIONS):
        owner_session = owner_session + (ends[s] <= page).astype(jnp.int32)
    mask = session == owner_session
    for j in range(heads):
        block = slice(j * lines, (j + 1) * lines)
        query = head_queries(queries, j, group)
        scores = lax.dot_general(
            query,
            fresh[:rows, j * HEAD_DIM : (j + 1) * HEAD_DIM],
            (((1,), (1,)), ((), ())),
            preferred_element_type=f32,
        )
        scores = jnp.where(mask, scores * HEAD_DIM ** (-0.5), floor_value)
        old = peak[block, :1]
        top = jnp.maximum(old, jnp.max(scores, axis=1, keepdims=True))
        weights = jnp.where(mask, jnp.exp(scores - top), 0.0)
        factor = jnp.exp(old - top)
        amount = total[block, :1] * factor + jnp.sum(weights, axis=1, keepdims=True)
        some = amount > 0.0
        divisor = jnp.where(some, amount, 1.0)
        weights_out[block, :] = weights.astype(bf16)
        level = jnp.where(some, top + jnp.log(divisor), floor_value)
        level_out[block, :] = jnp.broadcast_to(level, (lines, HEAD_DIM))
        mixed_out[block, :HEAD_DIM] = mixed[block, :] * factor
        mixed_out[block, HEAD_DIM:] = jnp.broadcast_to(1.0 / divisor, (lines, HEAD_DIM))


def values_kernel(heads, source, own, ahead, behind, scale, weights, levels, mixed, payload, fresh):
    sum_rows(own, ahead, behind, scale, fresh)
    lay_pages(source, fresh, payload)
    lines = weights.shape[0] // heads
    parts = []
    for j in range(heads):
        block = slice(j * lines, (j + 1) * lines)
        cols = slice(j * HEAD_DIM, (j + 1) * HEAD_DIM)
        part = mixed[block, :HEAD_DIM] + jnp.dot(
            weights[block, :], fresh[: own.shape[0], cols], preferred_element_type=f32
        )
        part = part * mixed[block, HEAD_DIM:]
        parts.append(part.astype(bf16).reshape(lines // PAGE, PAGE, HEAD_DIM))
    level = levels[...].T[:PAGE]
    high = level.astype(bf16).astype(f32)
    middle = (level - high).astype(bf16).astype(f32)
    low = level - high - middle
    line = lax.broadcasted_iota(jnp.int32, level.shape, 0)
    terms = jnp.where(line == 0, high, jnp.where(line == 1, middle, jnp.where(line == 2, low, 0.0)))
    terms = terms.astype(bf16)
    last = payload.shape[1] - 1
    first = last - lines // PAGE

    def spread(owner, carry):
        for j in range(heads):
            payload[owner, first:last, :, j * HEAD_DIM : (j + 1) * HEAD_DIM] = parts[j]
        payload[owner, last, :, :HEAD_DIM] = terms
        payload[owner, last, :, HEAD_DIM:] = jnp.zeros_like(payload[owner, last, :, HEAD_DIM:])
        return carry

    lax.fori_loop(0, payload.shape[0], spread, 0)


def last_kernel(key_pages, value_part, pages, out):
    owners, capacity, _, key_cols = key_pages.shape
    for i in range(owners):
        slots = slice(i * capacity, (i + 1) * capacity)
        pages[slots, :, :key_cols] = key_pages[i]
        pages[slots, :, key_cols:] = value_part[i, :capacity]
    steps = SESSIONS * STEPS
    heads = key_cols // HEAD_DIM
    last = value_part.shape[1] - 1
    rows = (last - capacity) * PAGE
    line = lax.broadcasted_iota(jnp.int32, (owners, HEAD_DIM), 0)
    level = jnp.zeros((owners, HEAD_DIM), f32)
    for i in range(owners):
        terms = value_part[i, last, :, :HEAD_DIM].astype(f32)
        level = jnp.where(line == i, terms[0:1] + terms[1:2] + terms[2:3], level)
    share = jnp.exp(level - jnp.max(level, axis=0, keepdims=True))
    share = share / jnp.sum(share, axis=0, keepdims=True)
    share = jnp.concatenate([share, jnp.zeros((HEAD_DIM - owners, HEAD_DIM), f32)], axis=0).T
    for j in range(heads):
        total = jnp.zeros((rows, HEAD_DIM), f32)
        for i in range(owners):
            part = value_part[i, capacity:last, :, j * HEAD_DIM : (j + 1) * HEAD_DIM]
            total = total + share[j * rows : (j + 1) * rows, i : i + 1] * part.reshape(rows, HEAD_DIM).astype(f32)
        result = total.astype(bf16)
        for g in range(rows // steps):
            column = (j * (rows // steps) + g) * HEAD_DIM
            out[:, column : column + HEAD_DIM] = result[g * steps : (g + 1) * steps, :]


def head_queries(queries, j, group):
    return jnp.concatenate(
        [queries[:, (j * group + g) * HEAD_DIM : (j * group + g + 1) * HEAD_DIM] for g in range(group)], axis=0
    )


def attend(state, query, keys, values, mask):
    peak, total, mixed = state
    scores = lax.dot_general(query, keys, (((1,), (1,)), ((), ())), preferred_element_type=f32)
    scores = jnp.where(mask, scores * HEAD_DIM ** (-0.5), floor_value)
    top = jnp.maximum(peak, jnp.max(scores, axis=1, keepdims=True))
    weights = jnp.where(mask, jnp.exp(scores - top), 0.0)
    factor = jnp.exp(peak - top)
    total = total * factor + jnp.sum(weights, axis=1, keepdims=True)
    mixed = mixed * factor + jnp.dot(weights.astype(bf16), values, preferred_element_type=f32)
    return top, total, mixed


def row_ids(rows, length):
    row = lax.broadcasted_iota(jnp.int32, (rows, length), 0) % (SESSIONS * STEPS)
    key = lax.broadcasted_iota(jnp.int32, (rows, length), 1)
    return row // STEPS, row % STEPS, key


def cache_kernel(where, lengths, early, queries, cache, new, after, peak_out, total_out, mixed_out):
    per_group = cache.shape[2] // (2 * HEAD_DIM)
    group = queries.shape[1] // (HEAD_DIM * per_group)
    rows = group * SESSIONS * STEPS
    local = cache.shape[1]
    ctx = where[0] * SIDE + where[1]
    for j in range(per_group):
        query = head_queries(queries, j, group)
        key_cols = slice(j * HEAD_DIM, (j + 1) * HEAD_DIM)
        value_cols = slice((per_group + j) * HEAD_DIM, (per_group + j + 1) * HEAD_DIM)
        state = (
            jnp.full((rows, 1), floor_value, f32),
            jnp.zeros((rows, 1), f32),
            jnp.zeros((rows, HEAD_DIM), f32),
        )
        for s in range(SESSIONS):
            session, step, key = row_ids(rows, local)
            mask = (session == s) & (key + ctx * local < lengths[s])
            state = attend(state, query, cache[s, :, key_cols], cache[s, :, value_cols], mask)
        session, step, key = row_ids(rows, new.shape[0])
        mask = (session == key // STEPS) & (key % STEPS <= step) & (ctx == 0)
        state = attend(state, query, new[:, key_cols], new[:, value_cols], mask)
        block = slice(j * rows, (j + 1) * rows)
        peak_out[block, :] = jnp.broadcast_to(state[0], (rows, HEAD_DIM))
        total_out[block, :] = jnp.broadcast_to(state[1], (rows, HEAD_DIM))
        mixed_out[block, :] = state[2]


def call(kernel, out_shape, in_specs, *operands, vmem=16, scratch=(), cost=NO_COST):
    return pl.pallas_call(
        kernel,
        out_shape=out_shape,
        in_specs=in_specs,
        out_specs=jax.tree.map(lambda _: VMEM, out_shape),
        scratch_shapes=scratch,
        compiler_params=pltpu.CompilerParams(vmem_limit_bytes=vmem * MEBI),
        cost_estimate=cost,
    )(*operands)


def per_device(
    layer_inputs, norm_gain, kv_weight, span_pages, page_owner, cache_len, cache_kv, queries, new_kv
):
    n_ctx = lax.axis_size("ctx")
    ctx_index = lax.axis_index("ctx")
    tp_index = lax.axis_index("tp")
    place = jnp.stack([ctx_index // SIDE, ctx_index % SIDE, tp_index]).astype(jnp.int32)
    own_part = layer_inputs[0]
    row_count, features = own_part.shape
    weight = kv_weight[0]
    kv_cols = weight.shape[1]
    shape = jax.ShapeDtypeStruct

    part_rows = features // SIDE
    one, three, band = call(
        pieces_kernel,
        [shape((part_rows, HEAD_DIM), bf16)] * 3,
        [SMEM, HBM],
        place,
        weight,
        scratch=[pltpu.SemaphoreType.DMA((3,))],
        cost=SOME_COST,
    )
    band = shift_tp(band, 2)
    near = jnp.stack([shift_tp(one, -1), shift_tp(three, 1)])
    pages_dev = row_count // PAGE
    capacity = max(2, 2 * pages_dev // n_ctx)
    owner = lax.dynamic_slice_in_dim(page_owner[:, 0], ctx_index * pages_dev, pages_dev)
    order = jnp.arange(pages_dev, dtype=jnp.int32)
    earlier = (owner[:, None] == owner[None, :]) & (order[None, :] < order[:, None])
    target = owner * capacity + jnp.sum(earlier.astype(jnp.int32), axis=1)
    slots = jnp.arange(n_ctx * capacity, dtype=jnp.int32)
    source = jnp.max(jnp.where(target[None, :] == slots[:, None], order[None, :], -1), axis=1)
    source = jnp.where(source < 0, pages_dev, source)
    ends = jnp.cumsum(span_pages)

    query = queries[0].reshape(SESSIONS * STEPS, -1)
    new = jnp.pad(new_kv[0].reshape(SESSIONS * STEPS, kv_cols), ((0, HEAD_DIM - SESSIONS * STEPS), (0, 0)))
    state_shape = shape((query.shape[1] // HEAD_DIM * SESSIONS * STEPS, HEAD_DIM), f32)

    band_x = [from_x(band, k) for k in range(1, SIDE)]
    near_y = [from_y(near, k) for k in range(1, SIDE)]
    far_column, gathered = call(
        functools.partial(rows_kernel, 0),
        [shape((features, HEAD_DIM), bf16), TOKEN],
        [SMEM] + [VMEM] * (2 * SIDE - 1),
        place,
        band,
        *band_x,
        *near_y,
    )
    near_column, _ = call(
        functools.partial(rows_kernel, 1),
        [shape((2, features, HEAD_DIM), bf16), TOKEN],
        [SMEM] + [VMEM] * SIDE,
        place,
        near,
        *near_y,
    )
    far_parts = [far_column] + [from_y(far_column, k) for k in range(1, SIDE)]
    state = call(
        cache_kernel,
        [state_shape] * 3,
        [SMEM, SMEM, SMEM, VMEM, VMEM, VMEM, VMEM],
        place,
        cache_len,
        source,
        query,
        cache_kv[0],
        new,
        gathered,
    )
    near_x = [from_x(near_column, k) for k in range(1, SIDE)]

    inner = lax.ppermute(own_part, "section", [(0, 1), (2, 3)])
    chip = add_after(inner, own_part, band, near)
    crossed = lax.ppermute(chip, "section", [(1, 2)])
    crossed = tied(crossed, state[0], near_column, *far_parts)
    passed = lax.ppermute(crossed, "section", [(2, 3)])

    info = jnp.concatenate([place, lax.axis_index("section").astype(jnp.int32)[None]])
    hs, squares = hidden_state(info, chip, crossed, passed, norm_gain)

    cut = row_count // 2
    far_low, far_high, far_done = call(
        far_kernel,
        [shape((cut + 16, kv_cols), bf16), shape((row_count - cut, kv_cols), bf16), TOKEN],
        [SMEM, VMEM, VMEM] + [VMEM] * SIDE,
        place,
        squares,
        hs,
        *far_parts,
        scratch=[pltpu.VMEM((features, kv_cols), bf16), pltpu.SemaphoreType.DMA((SIDE,))],
    )
    key_cols = kv_cols // 2
    own = call(
        own_kernel,
        [shape((row_count, width), f32) for width in (key_cols, kv_cols - key_cols)] + [TOKEN],
        [VMEM, HBM, SMEM, VMEM],
        hs,
        weight,
        place,
        far_done,
        scratch=[pltpu.VMEM((features, kv_cols), bf16), pltpu.SemaphoreType.DMA],
    )
    near_weight = call(
        columns_kernel,
        shape((features, 2 * kv_cols), bf16),
        [SMEM] + [VMEM] * (SIDE + 1),
        place,
        near_column,
        *near_x,
        own[2],
    )
    passing = (shift_tp(far_low, 1), shift_tp(far_high, -1))
    ahead, behind, ahead_values, behind_values, near_done = call(
        functools.partial(near_kernel, [key_cols, kv_cols - key_cols]),
        [shape((row_count + 16, key_cols), bf16)] * 2
        + [shape((row_count, kv_cols - key_cols), bf16)] * 2
        + [TOKEN],
        [VMEM] * 5,
        squares,
        hs,
        near_weight,
        *passing,
        vmem=24,
    )
    key_sums = (shift_tp(ahead, 1), shift_tp(behind, -1))
    token = call(token_kernel, TOKEN, [VMEM] * 2, *key_sums)
    token = lax.ppermute(token, "section", [(0, 1), (1, 0), (2, 3), (3, 2)])
    ahead, behind = tied_pair(ahead_values, behind_values, token)
    value_sums = (shift_tp(ahead, 1), shift_tp(behind, -1))

    heads = key_cols // HEAD_DIM
    state_rows = state_shape.shape[0]

    def send_keys(squares, own_keys, ahead, behind, state):
        scale, fresh, pages, weights, levels, mixed = call(
            functools.partial(keys_kernel, heads),
            [
                TOKEN,
                shape((row_count + PAGE, key_cols), bf16),
                shape((n_ctx, capacity, PAGE, key_cols), bf16),
                shape((state_rows, row_count), bf16),
                state_shape,
                shape((state_rows, 2 * HEAD_DIM), f32),
            ],
            [SMEM] * 3 + [VMEM] * 8,
            place,
            ends,
            source,
            squares,
            own_keys,
            ahead,
            behind,
            query,
            *state,
        )
        pages = lax.all_to_all(pages, "ctx", split_axis=0, concat_axis=0, tiled=True)
        return pages, scale, weights, levels, mixed

    def send_none(squares, own_keys, ahead, behind, state):
        return (
            jnp.zeros((n_ctx, capacity, PAGE, key_cols), bf16),
            squares,
            jnp.zeros((state_rows, row_count), bf16),
            state[0],
            jnp.zeros((state_rows, 2 * HEAD_DIM), f32),
        )

    key_pages, scale, weights, levels, mixed = lax.cond(
        span_pages[0] >= 0, send_keys, send_none, squares, own[0], *key_sums, state
    )
    payload = call(
        functools.partial(values_kernel, heads),
        shape((n_ctx, capacity + state_rows // heads // PAGE + 1, PAGE, kv_cols - key_cols), bf16),
        [SMEM] + [VMEM] * 7,
        source,
        own[1],
        *value_sums,
        scale,
        weights,
        levels,
        mixed,
        scratch=[pltpu.VMEM((row_count + PAGE, kv_cols - key_cols), bf16)],
    )
    value_part = lax.all_to_all(payload, "ctx", split_axis=0, concat_axis=0, tiled=True)
    page_store, attention = call(
        last_kernel,
        [shape((n_ctx * capacity, PAGE, kv_cols), bf16), shape(query.shape, bf16)],
        [VMEM] * 2,
        key_pages,
        value_part,
    )
    return (page_store[None], attention.reshape(1, SESSIONS, STEPS, -1))


def solution(mesh):
    return jax.shard_map(
        per_device,
        mesh=mesh,
        in_specs=(
            P("section", "ctx", "tp"),
            P("section", "tp"),
            P("section", None, "tp"),
            P(),
            P(),
            P(),
            P("section", None, "ctx", "tp"),
            P("section", None, None, "tp"),
            P("section", None, None, "tp"),
        ),
        out_specs=(P("section", "ctx", None, "tp"), P("section", None, None, "tp")),
        check_vma=False,
    )
```

time: 227 us -> 195 us (0.86)
  blocking collectives: 19.1 us -> 54 us
  waiting for transfers between devices: 80.4 us -> 52.1 us
  starting transfers between devices: 59.1 us -> 41 us
  local copies, waits for them, and re-layouts: 20.8 us -> 12.1 us
  Pallas kernels: 36.6 us -> 31 us
  other arithmetic: 6.13 us -> 1.35 us
    all_to_all x0 -> x1, blocking collectives: none -> 27.8 us  [send_keys(): lax.all_to_all(pages, 'ctx', split_axis=0, concat_axis=0, tiled=True)]
    ppermute x14 -> x9, waiting for transfers between devices: 38.1 us -> 24.7 us  [shift_tp(): lax.ppermute(array, 'tp', [(i, (i + by) % peers) for i in range(peers)])]
    ppermute x6, waiting for transfers between devices: 18 us -> 5.29 us  [from_y(): return lax.ppermute(array, 'ctx', pairs)]
    all_to_all x2 -> x0, starting transfers between devices: 11.2 us -> none  [the longest x1 6.81 us: per_device(): lax.all_to_all(payload, 'ctx', split_axis=0, concat_axis=0, tiled=True)]
    unnamed x74 -> x54, local copies, waits for them, and re-layouts: 19.2 us -> 8.55 us
    pallas_call x13 -> x12, Pallas kernels: 33.9 us -> 24.2 us  [call(): pl.pallas_call(kernel, out_shape=out_shape, in_specs=in_specs, out_specs=...]
    ppermute x14 -> x9, starting transfers between devices: 26.4 us -> 18.5 us  [shift_tp(): lax.ppermute(array, 'tp', [(i, (i + by) % peers) for i in range(peers)])]
    all_to_all x1, blocking collectives: 19.1 us -> 26.1 us  [per_device(): lax.all_to_all(payload, 'ctx', split_axis=0, concat_axis=0, tiled=True)]
  transfers between devices with their start and end apart: 31 -> 25, of which waited for: 13 -> 9; matrix products, arithmetic and copies ran while one was open for 3% -> 2% of each run, Pallas kernels for 11% -> 11%
where the time goes in v2:
time: 195 us; the launch traced here: 192 us
  blocking collectives  54 us (28%)
  waiting for transfers between devices  52.1 us (27%)
  starting transfers between devices  41 us (21%)
  Pallas kernels  31 us (16%)
  local copies, waits for them, and re-layouts  12.1 us (6%)
    all_to_all x1, blocking collectives, send_keys(): lax.all_to_all(pages, 'ctx', split_axis=0, concat_axis=0, tiled=True)  27.8 us
    all_to_all x1, blocking collectives, per_device(): lax.all_to_all(payload, 'ctx', split_axis=0, concat_axis=0, tiled=True)  26.1 us
    ppermute x9, waiting for transfers between devices, shift_tp(): lax.ppermute(array, 'tp', [(i, (i + by) % peers) for i in range(peers)])  24.7 us
    pallas_call x12, Pallas kernels, call(): pl.pallas_call(kernel, out_shape=out_shape, in_specs=in_specs, out_specs=...  24.2 us
    ppermute x6, waiting for transfers between devices, from_x(): return lax.ppermute(array, 'ctx', pairs)  20.9 us
    ppermute x9, starting transfers between devices, shift_tp(): lax.ppermute(array, 'tp', [(i, (i + by) % peers) for i in range(peers)])  18.5 us
    ppermute x6, starting transfers between devices, from_y(): return lax.ppermute(array, 'ctx', pairs)  9.48 us
    unnamed x54, local copies, waits for them, and re-layouts  8.55 us
  transfers between devices with their start and end apart: 25, of which 9 were waited for; matrix products, arithmetic and copies ran while one was open for 2% of the time, Pallas kernels for 11%

profile of v2, /device:TPU:64, one launch (start us, length us, event | category | flops | bytes accessed | tf_op | source)
XLA Modules:
  0.0 192.5 jit_solution(25931964877733834)
XLA Ops:
  0.6 1.9 collective-permute-start
  2.6 0.1 pad_add_fusion.1.place.where
  2.6 2.5 %copy-done = bf16[1,5120,512]{2,1,0:T(8,128)(2,1)S(1)} copy-done((bf16[1,5120,512]{2,1,0:T(8,128)(2,1)S(1)}, bf16[1,5120,512]{2,1,0:T(8,128)(2,1)}, u32[]{:S(2)}) %copy-start) | copy-done | bytes 5242904
  5.1 0.6 shard_map.104
  5.8 1.0 collective-permute-start.2
  6.8 3.6 %collective-permute-start.3 = (bf16[320,128]{1,0:T(8,128)(2,1)S(1)}, bf16[320,128]{1,0:T(8,128)(2,1)S(1)}, u32[]{:S(2)}, u32[]{:S(2)}) collective-permute-start(bf16[320,128]{1,0:T(8,128)(2,1)S(1)} %get-tuple-element.79), channel_id=1, source_target_pairs={{0,1},{1,2},{2,3},{3,0},{4,5},{5,6},{6,7},{7,4},{8,9},{9,10},{10,1... | collective-permute-start | bytes 245768 | tf_op jit(solution)/shard_map/ppermute | solution.py:33
  10.4 5.0 %collective-permute-start.1 = (bf16[320,128]{1,0:T(8,128)(2,1)S(1)}, bf16[320,128]{1,0:T(8,128)(2,1)S(1)}, u32[]{:S(2)}, u32[]{:S(2)}) collective-permute-start(bf16[320,128]{1,0:T(8,128)(2,1)S(1)} %get-tuple-element.77), channel_id=1, source_target_pairs={{0,2},{1,3},{2,0},{3,1},{4,6},{5,7},{6,4},{7,5},{8,10},{9,11},{10,... | collective-permute-start | bytes 245768 | tf_op jit(solution)/shard_map/ppermute | solution.py:33
  15.4 5.9 %collective-permute-done.1.refs_0_ = bf16[320,128]{1,0:T(8,128)(2,1)S(1)} collective-permute-done((bf16[320,128]{1,0:T(8,128)(2,1)S(1)}, bf16[320,128]{1,0:T(8,128)(2,1)S(1)}, u32[]{:S(2)}, u32[]{:S(2)}) %collective-permute-start.1) | collective-permute-done | bytes 81952 | tf_op jit(solution)/shard_map/ppermute | solution.py:33
  21.4 2.2 %shard_map.105.chip = bf16[1024,1280]{1,0:T(8,128)(2,1)} custom-call(bf16[1024,1280]{1,0:T(8,128)(2,1)S(1)} %collective-permute-done.first, bf16[1024,1280]{1,0:T(8,128)(2,1)S(1)} %bitcast.24, bf16[320,128]{1,0:T(8,128)(2,1)S(1)} %collective-permute-done.1.refs_0_, bf16[2,320,128]{2,1,0:T(8,128)(2,1)S(1)} %pad_maximum_fusion.refs_1_.refs_0_), custom_call_target="tpu_custom_call" | custom-call | flops 8000000000 | tf_op jit(solution)/shard_map/pallas_call | solution.py:57
  23.6 0.8 collective-permute-start.4
  24.4 0.7 dynamic-slice_bitcast_fusion
  25.2 2.8 %collective-permute-start.5 = (bf16[320,128]{1,0:T(8,128)(2,1)S(1)}, bf16[320,128]{1,0:T(8,128)(2,1)S(1)}, u32[]{:S(2)}, u32[]{:S(2)}) collective-permute-start(bf16[320,128]{1,0:T(8,128)(2,1)S(1)} %collective-permute-done.1.refs_0_), channel_id=1, source_target_pairs={{16,0},{20,4},{24,8},{28,12},{32,16},{36,20},{40,24},{44,28},{48,3... | collective-permute-start | bytes 245768 | tf_op jit(solution)/shard_map/ppermute | solution.py:38
  27.9 0.8 collective-permute-start.6
  28.7 0.2 convert_reduce_fusion
  28.9 1.7 collective-permute-start.10
  30.5 1.7 collective-permute-start.8
  32.2 3.2 %collective-permute-start.9 = (bf16[2,320,128]{2,1,0:T(8,128)(2,1)S(1)}, bf16[2,320,128]{2,1,0:T(8,128)(2,1)S(1)}, u32[]{:S(2)}, u32[]{:S(2)}) collective-permute-start(bf16[2,320,128]{2,1,0:T(8,128)(2,1)S(1)} %pad_maximum_fusion.refs_1_.refs_0_), channel_id=1, source_target_pairs={{8,0},{12,4},{0,8},{4,12},{24,16},{28,20},{16,24},{20,28},{40,32},... | collective-permute-start | bytes 491528 | tf_op jit(solution)/shard_map/ppermute | solution.py:43
  35.4 0.7 multiply_add_fusion
  36.1 1.4 reshape_squeeze.6.queries
  37.5 0.7 reshape_squeeze.7
  38.3 3.3 %collective-permute-done.7.refs_3_ = bf16[320,128]{1,0:T(8,128)(2,1)} collective-permute-done((bf16[320,128]{1,0:T(8,128)(2,1)S(1)}, bf16[320,128]{1,0:T(8,128)(2,1)}, u32[]{:S(2)}, u32[]{:S(2)}) %collective-permute-start.7) | collective-permute-done | bytes 81952 | tf_op jit(solution)/shard_map/ppermute | solution.py:38
  41.6 1.0 shard_map.106
  42.7 1.4 collective-permute-start.11
  44.1 1.4 collective-permute-start.12
  45.5 0.2 collective-permute-start.13
  45.7 0.1 select_reduce_fusion
  45.8 1.6 copy-done.1
  47.4 4.0 %shard_map.107 = (f32[128,128]{1,0:T(8,128)S(1)}, f32[128,128]{1,0:T(8,128)}, f32[128,128]{1,0:T(8,128)}) custom-call(s32[3]{0:T(128)S(1)} %pad_add_fusion.1.place.where, s32[4]{0:T(128)S(1)} %copy-done.16, s32[128]{0:T(128)S(1)} %compare_select_fusion.early.source, bf16[16,1024]{1,0:T(8,128)(2,1)} %reshape_squeeze.6.queries, ...), custom_call_target="tpu_custom_call" | custom-call | tf_op jit(solution)/shard_map/pallas_call | solution.py:452
  51.4 0.9 copy-done.11
  52.3 0.9 copy-done.13
  53.2 0.9 copy-done.15
  54.1 1.1 shard_map.108
  55.3 1.0 collective-permute-done.12.refs_5_.refs_2_
  56.3 4.3 %collective-permute-done.13.refs_6_.refs_3_ = bf16[1280,128]{1,0:T(8,128)(2,1)S(1)} collective-permute-done((bf16[1280,128]{1,0:T(8,128)(2,1)S(1)}, bf16[1280,128]{1,0:T(8,128)(2,1)S(1)}, u32[]{:S(2)}, u32[]{:S(2)}) %collective-permute-start.13) | collective-permute-done | bytes 327712 | tf_op jit(solution)/shard_map/ppermute | solution.py:43
  60.6 0.7 copy-done.8
  61.3 2.2 %collective-permute-start.14 = (bf16[1024,1280]{1,0:T(8,128)(2,1)S(1)}, bf16[1024,1280]{1,0:T(8,128)(2,1)}, u32[]{:S(2)}, u32[]{:S(2)}) collective-permute-start(bf16[1024,1280]{1,0:T(8,128)(2,1)S(1)} %shard_map.109.crossed), channel_id=1, source_target_pairs={{128,192},{129,193},{130,194},{131,195},{132,196},{133,197},{134,1... | collective-permute-start | bytes 7864328 | tf_op jit(solution)/shard_map/ppermute | solution.py:541
  63.4 0.1 pad_add_fusion.info
  63.5 0.0 slice-start.1
  63.5 3.6 %collective-permute-start.15 = (bf16[2,1280,128]{2,1,0:T(8,128)(2,1)S(1)}, bf16[2,1280,128]{2,1,0:T(8,128)(2,1)S(1)}, u32[]{:S(2)}, u32[]{:S(2)}) collective-permute-start(bf16[2,1280,128]{2,1,0:T(8,128)(2,1)S(1)} %get-tuple-element.82.refs_2_.refs_0_), channel_id=1, source_target_pairs={{16,0},{20,4},{24,8},{28,12},{32,16},{36,20},{40,24},{44,28},{48,3... | collective-permute-start | bytes 1966088 | tf_op jit(solution)/shard_map/ppermute | solution.py:38
  67.2 1.0 collective-permute-start.17
  68.1 4.5 %shard_map.110 = (bf16[1024,1280]{1,0:T(8,128)(2,1)S(1)}, f32[8,128]{1,0:T(8,128)S(1)}) custom-call(s32[4]{0:T(128)S(1)} %pad_add_fusion.info, bf16[1024,1280]{1,0:T(8,128)(2,1)} %shard_map.105.chip, bf16[1024,1280]{1,0:T(8,128)(2,1)S(1)} %shard_map.109.crossed, bf16[1024,1280]{1,0:T(8,128)(2,1)} %collective-permute-done.14.passed, ...), custom_call_target="tpu_custom_call" | custom-call | flops 8000000000 | tf_op jit(solution)/shard_map/pallas_call | solution.py:212
  72.6 2.3 %shard_map.111 = (bf16[528,512]{1,0:T(8,128)(2,1)S(1)}, bf16[512,512]{1,0:T(8,128)(2,1)S(1)}, f32[8,128]{1,0:T(8,128)S(1)}) custom-call(s32[3]{0:T(128)S(1)} %pad_add_fusion.1.place.where, f32[8,128]{1,0:T(8,128)S(1)} %get-tuple-element.84.squares, bf16[1024,1280]{1,0:T(8,128)(2,1)S(1)} %get-tuple-element.85.hs, bf16[1280,128]{1,0:T(8,128)(2,1)S(1)} %copy-done.3, ...), custom_call_target="tpu_custom_call" | custom-call | tf_op jit(solution)/shard_map/pallas_call | solution.py:452
  75.0 3.0 %collective-permute-start.18 = (bf16[528,512]{1,0:T(8,128)(2,1)S(1)}, bf16[528,512]{1,0:T(8,128)(2,1)S(1)}, u32[]{:S(2)}, u32[]{:S(2)}) collective-permute-start(bf16[528,512]{1,0:T(8,128)(2,1)S(1)} %get-tuple-element.89), channel_id=1, source_target_pairs={{0,1},{1,2},{2,3},{3,0},{4,5},{5,6},{6,7},{7,4},{8,9},{9,10},{10,1... | collective-permute-start | bytes 1622024 | tf_op jit(solution)/shard_map/ppermute | solution.py:33
  78.0 3.1 %shard_map.112 = (f32[1024,256]{1,0:T(8,128)}, f32[1024,256]{1,0:T(8,128)S(1)}, f32[8,128]{1,0:T(8,128)S(1)}) custom-call(bf16[1024,1280]{1,0:T(8,128)(2,1)S(1)} %get-tuple-element.85.hs, bf16[5120,512]{1,0:T(8,128)(2,1)S(1)} %bitcast.21, s32[3]{0:T(128)S(1)} %pad_add_fusion.1.place.where, f32[8,128]{1,0:T(8,128)S(1)} %get-tuple-element.86.after), custom_call_target="tpu_custom_call" | custom-call | tf_op jit(solution)/shard_map/pallas_call | solution.py:452
  81.2 14.2 %collective-permute-done.15.refs_1_ = bf16[2,1280,128]{2,1,0:T(8,128)(2,1)S(1)} collective-permute-done((bf16[2,1280,128]{2,1,0:T(8,128)(2,1)S(1)}, bf16[2,1280,128]{2,1,0:T(8,128)(2,1)S(1)}, u32[]{:S(2)}, u32[]{:S(2)}) %collective-permute-start.15) | collective-permute-done | bytes 655392 | tf_op jit(solution)/shard_map/ppermute | solution.py:38
  95.4 3.4 %collective-permute-done.17.refs_3_ = bf16[2,1280,128]{2,1,0:T(8,128)(2,1)S(1)} collective-permute-done((bf16[2,1280,128]{2,1,0:T(8,128)(2,1)S(1)}, bf16[2,1280,128]{2,1,0:T(8,128)(2,1)S(1)}, u32[]{:S(2)}, u32[]{:S(2)}) %collective-permute-start.17) | collective-permute-done | bytes 655392 | tf_op jit(solution)/shard_map/ppermute | solution.py:38
  98.8 1.3 shard_map.113.weight
  100.1 3.4 %shard_map.114 = (bf16[1040,256]{1,0:T(8,128)(2,1)S(1)}, bf16[1040,256]{1,0:T(8,128)(2,1)S(1)}, bf16[1024,256]{1,0:T(8,128)(2,1)S(1)}, bf16[1024,256]{1,0:T(8,128)(2,1)S(1)}, f32[8,128]{1,0:T(8,128)}) custom-call(f32[8,128]{1,0:T(8,128)S(1)} %get-tuple-element.84.squares, bf16[1024,1280]{1,0:T(8,128)(2,1)S(1)} %get-tuple-element.85.hs, ...), custom_call_target="tpu_custom_call" | custom-call | tf_op jit(solution)/shard_map/pallas_call | solution.py:452
  103.5 1.2 collective-permute-start.20
  104.7 1.7 collective-permute-start.21
  106.4 15.2 %collective-permute-done.20.refs_0_ = bf16[1040,256]{1,0:T(8,128)(2,1)S(1)} collective-permute-done((bf16[1040,256]{1,0:T(8,128)(2,1)S(1)}, bf16[1040,256]{1,0:T(8,128)(2,1)S(1)}, u32[]{:S(2)}, u32[]{:S(2)}) %collective-permute-start.20) | collective-permute-done | bytes 532512 | tf_op jit(solution)/shard_map/ppermute | solution.py:33
  121.6 3.5 %collective-permute-done.21.refs_1_ = bf16[1040,256]{1,0:T(8,128)(2,1)S(1)} collective-permute-done((bf16[1040,256]{1,0:T(8,128)(2,1)S(1)}, bf16[1040,256]{1,0:T(8,128)(2,1)S(1)}, u32[]{:S(2)}, u32[]{:S(2)}) %collective-permute-start.21) | collective-permute-done | bytes 532512 | tf_op jit(solution)/shard_map/ppermute | solution.py:33
  125.2 1.2 collective-permute-done.22.refs_2_
  126.3 0.6 collective-permute-start.23
  126.9 2.4 %collective-permute-start.24 = (bf16[1024,256]{1,0:T(8,128)(2,1)S(1)}, bf16[1024,256]{1,0:T(8,128)(2,1)S(1)}, u32[]{:S(2)}, u32[]{:S(2)}) collective-permute-start(bf16[1024,256]{1,0:T(8,128)(2,1)S(1)} %get-tuple-element.100), channel_id=1, source_target_pairs={{0,3},{1,0},{2,1},{3,2},{4,7},{5,4},{6,5},{7,6},{8,11},{9,8},{10,9... | collective-permute-start | bytes 1572872 | tf_op jit(solution)/shard_map/ppermute | solution.py:33
  129.3 0.2 reduce-window.6
  129.5 31.4 %conditional.1 = (bf16[16,8,16,256]{3,2,1,0:T(8,128)(2,1)S(1)}, f32[8,128]{1,0:T(8,128)S(1)}, bf16[128,1024]{1,0:T(8,128)(2,1)S(1)}, f32[128,128]{1,0:T(8,128)S(1)}, f32[128,256]{1,0:T(8,128)}) conditional(s32[]{:T(128)} %bitcast.1, (f32[8,128]{1,0:T(8,128)S(1)}, f32[128,128]{1,0:T(8,128)S(1)}) %tuple.16, (s32[4,1]{0,1:T(1,128)S(1)}, s32[3]{0:T(128)S(1)}, ...), branch_computations={%region_3.4_spmd, %region_4.5_spmd} | conditional | bytes 2236456 | solution.py:633
  129.5 3.5 %branch_1_fun.1 = (f32[8,128]{1,0:T(8,128)S(1)}, bf16[1040,256]{1,0:T(8,128)(2,1)}, bf16[16,8,16,256]{3,2,1,0:T(8,128)(2,1)S(1)}, bf16[128,1024]{1,0:T(8,128)(2,...) custom-call(s32[3]{0:T(128)S(1)} %get-tuple-element.29.place, s32[4]{0:T(128)S(1)} %bitcast.27, ...), custom_call_target="tpu_custom_call" | custom-call | tf_op jit(solution)/shard_map/cond/branch_1_fun/pallas_call | solution.py:452
  133.1 27.8 %all_to_all.9 = bf16[16,8,16,256]{3,2,1,0:T(8,128)(2,1)S(1)} all-to-all(bf16[16,8,16,256]{3,2,1,0:T(8,128)(2,1)S(1)} %get-tuple-element.40), channel_id=1, replica_groups=mesh['section'=4,'ctx'=16,'tp'=4] {'ctx'}, dimensions={0} | all-to-all | bytes 2097152 | tf_op jit(solution)/shard_map/cond/branch_1_fun/all_to_all | solution.py:621
  160.9 1.0 copy-done.19
  161.9 1.9 shard_map.117
  163.8 26.1 %all_to_all.10.value_part = bf16[16,13,16,256]{3,2,1,0:T(8,128)(2,1)S(1)} all-to-all(bf16[16,13,16,256]{3,2,1,0:T(8,128)(2,1)S(1)} %shard_map.117), channel_id=1, replica_groups=mesh['section'=4,'ctx'=16,'tp'=4] {'ctx'}, dimensions={0} | all-to-all | bytes 3407872 | tf_op jit(solution)/shard_map/all_to_all | solution.py:649
  189.9 1.9 %shard_map.118 = (bf16[128,16,512]{2,1,0:T(8,128)(2,1)}, bf16[16,1024]{1,0:T(8,128)(2,1)S(1)}) custom-call(bf16[16,8,16,256]{3,2,1,0:T(8,128)(2,1)S(1)} %copy-done.20, bf16[16,13,16,256]{3,2,1,0:T(8,128)(2,1)S(1)} %all_to_all.10.value_part), custom_call_target="tpu_custom_call" | custom-call | tf_op jit(solution)/shard_map/pallas_call | solution.py:452
  191.8 0.6 reshape.36
  (75 shorter events, 0.2 us)
Async XLA Ops:
  0.6 20.7 %collective-permute-start = (bf16[1024,1280]{1,0:T(8,128)(2,1)}, bf16[1024,1280]{1,0:T(8,128)(2,1)S(1)}, u32[]{:S(2)}, u32[]{:S(2)}) collective-permute-start(bf16[1024,1280]{1,0:T(8,128)(2,1)} %bitcast.23), channel_id=1, source_target_pairs={{0,64},{128,192},{1,65},{129,193},{2,66},{130,194},{3,67},{131,195... | collective-permute-start | bytes 7864328 | tf_op jit(solution)/shard_map/ppermute | solution.py:537
  2.6 2.5 %copy-start = (bf16[1,5120,512]{2,1,0:T(8,128)(2,1)S(1)}, bf16[1,5120,512]{2,1,0:T(8,128)(2,1)}, u32[]{:S(2)}) copy-start(bf16[1,5120,512]{2,1,0:T(8,128)(2,1)} %param.13) | copy-start | bytes 15728644
  5.1 16.2 %copy-start.17 = (bf16[1,1024,1280]{2,1,0:T(8,128)(2,1)S(1)}, bf16[1,1024,1280]{2,1,0:T(8,128)(2,1)}, u32[]{:S(2)}) copy-start(bf16[1,1024,1280]{2,1,0:T(8,128)(2,1)} %param.11) | copy-start | bytes 7864324
  5.8 9.6 %collective-permute-start.2 = (bf16[320,128]{1,0:T(8,128)(2,1)S(1)}, bf16[320,128]{1,0:T(8,128)(2,1)S(1)}, u32[]{:S(2)}, u32[]{:S(2)}) collective-permute-start(bf16[320,128]{1,0:T(8,128)(2,1)S(1)} %get-tuple-element.78), channel_id=1, source_target_pairs={{0,3},{1,0},{2,1},{3,2},{4,7},{5,4},{6,5},{7,6},{8,11},{9,8},{10,9... | collective-permute-start | bytes 245768 | tf_op jit(solution)/shard_map/ppermute | solution.py:33
  6.8 8.6 %collective-permute-start.3 = (bf16[320,128]{1,0:T(8,128)(2,1)S(1)}, bf16[320,128]{1,0:T(8,128)(2,1)S(1)}, u32[]{:S(2)}, u32[]{:S(2)}) collective-permute-start(bf16[320,128]{1,0:T(8,128)(2,1)S(1)} %get-tuple-element.79), channel_id=1, source_target_pairs={{0,1},{1,2},{2,3},{3,0},{4,5},{5,6},{6,7},{7,4},{8,9},{9,10},{10,1... | collective-permute-start | bytes 245768 | tf_op jit(solution)/shard_map/ppermute | solution.py:33
  10.4 10.9 %collective-permute-start.1 = (bf16[320,128]{1,0:T(8,128)(2,1)S(1)}, bf16[320,128]{1,0:T(8,128)(2,1)S(1)}, u32[]{:S(2)}, u32[]{:S(2)}) collective-permute-start(bf16[320,128]{1,0:T(8,128)(2,1)S(1)} %get-tuple-element.77), channel_id=1, source_target_pairs={{0,2},{1,3},{2,0},{3,1},{4,6},{5,7},{6,4},{7,5},{8,10},{9,11},{10,... | collective-permute-start | bytes 245768 | tf_op jit(solution)/shard_map/ppermute | solution.py:33
  15.4 30.4 %copy-start.16 = (s32[4]{0:T(128)S(1)}, s32[4]{0:T(128)}, u32[]{:S(2)}) copy-start(s32[4]{0:T(128)} %lengths.1) | copy-start | bytes 52
  23.6 37.0 %collective-permute-start.4 = (bf16[1024,1280]{1,0:T(8,128)(2,1)}, bf16[1024,1280]{1,0:T(8,128)(2,1)S(1)}, u32[]{:S(2)}, u32[]{:S(2)}) collective-permute-start(bf16[1024,1280]{1,0:T(8,128)(2,1)} %shard_map.105.chip), channel_id=1, source_target_pairs={{64,128},{65,129},{66,130},{67,131},{68,132},{69,133},{70,134},{71... | collective-permute-start | bytes 7864328 | tf_op jit(solution)/shard_map/ppermute | solution.py:539
  25.2 7.1 %collective-permute-start.5 = (bf16[320,128]{1,0:T(8,128)(2,1)S(1)}, bf16[320,128]{1,0:T(8,128)(2,1)S(1)}, u32[]{:S(2)}, u32[]{:S(2)}) collective-permute-start(bf16[320,128]{1,0:T(8,128)(2,1)S(1)} %collective-permute-done.1.refs_0_), channel_id=1, source_target_pairs={{16,0},{20,4},{24,8},{28,12},{32,16},{36,20},{40,24},{44,28},{48,3... | collective-permute-start | bytes 245768 | tf_op jit(solution)/shard_map/ppermute | solution.py:38
  27.9 7.5 %collective-permute-start.6 = (bf16[320,128]{1,0:T(8,128)(2,1)S(1)}, bf16[320,128]{1,0:T(8,128)(2,1)S(1)}, u32[]{:S(2)}, u32[]{:S(2)}) collective-permute-start(bf16[320,128]{1,0:T(8,128)(2,1)S(1)} %collective-permute-done.1.refs_0_), channel_id=1, source_target_pairs={{32,0},{36,4},{40,8},{44,12},{48,16},{52,20},{56,24},{60,28},{0,32... | collective-permute-start | bytes 245768 | tf_op jit(solution)/shard_map/ppermute | solution.py:38
  28.9 12.7 %collective-permute-start.10 = (bf16[2,320,128]{2,1,0:T(8,128)(2,1)S(1)}, bf16[2,320,128]{2,1,0:T(8,128)(2,1)S(1)}, u32[]{:S(2)}, u32[]{:S(2)}) collective-permute-start(bf16[2,320,128]{2,1,0:T(8,128)(2,1)S(1)} %pad_maximum_fusion.refs_1_.refs_0_), channel_id=1, source_target_pairs={{12,0},{0,4},{4,8},{8,12},{28,16},{16,20},{20,24},{24,28},{44,32},... | collective-permute-start | bytes 491528 | tf_op jit(solution)/shard_map/ppermute | solution.py:43
  30.5 11.0 %collective-permute-start.8 = (bf16[2,320,128]{2,1,0:T(8,128)(2,1)S(1)}, bf16[2,320,128]{2,1,0:T(8,128)(2,1)S(1)}, u32[]{:S(2)}, u32[]{:S(2)}) collective-permute-start(bf16[2,320,128]{2,1,0:T(8,128)(2,1)S(1)} %pad_maximum_fusion.refs_1_.refs_0_), channel_id=1, source_target_pairs={{4,0},{8,4},{12,8},{0,12},{20,16},{24,20},{28,24},{16,28},{36,32},... | collective-permute-start | bytes 491528 | tf_op jit(solution)/shard_map/ppermute | solution.py:43
  32.2 9.4 %collective-permute-start.9 = (bf16[2,320,128]{2,1,0:T(8,128)(2,1)S(1)}, bf16[2,320,128]{2,1,0:T(8,128)(2,1)S(1)}, u32[]{:S(2)}, u32[]{:S(2)}) collective-permute-start(bf16[2,320,128]{2,1,0:T(8,128)(2,1)S(1)} %pad_maximum_fusion.refs_1_.refs_0_), channel_id=1, source_target_pairs={{8,0},{12,4},{0,8},{4,12},{24,16},{28,20},{16,24},{20,28},{40,32},... | collective-permute-start | bytes 491528 | tf_op jit(solution)/shard_map/ppermute | solution.py:43
  35.4 6.2 %collective-permute-start.7 = (bf16[320,128]{1,0:T(8,128)(2,1)S(1)}, bf16[320,128]{1,0:T(8,128)(2,1)}, u32[]{:S(2)}, u32[]{:S(2)}) collective-permute-start(bf16[320,128]{1,0:T(8,128)(2,1)S(1)} %collective-permute-done.1.refs_0_), channel_id=1, source_target_pairs={{48,0},{52,4},{56,8},{60,12},{0,16},{4,20},{8,24},{12,28},{16,32},... | collective-permute-start | bytes 245768 | tf_op jit(solution)/shard_map/ppermute | solution.py:38
  41.6 4.2 %copy-start.10 = (bf16[2,320,128]{2,1,0:T(8,128)(2,1)}, bf16[2,320,128]{2,1,0:T(8,128)(2,1)S(1)}, u32[]{:S(2)}) copy-start(bf16[2,320,128]{2,1,0:T(8,128)(2,1)S(1)} %collective-permute-done.10.refs_6_.refs_3_) | copy-start | bytes 491524
  41.6 4.2 %copy-start.12 = (bf16[2,320,128]{2,1,0:T(8,128)(2,1)}, bf16[2,320,128]{2,1,0:T(8,128)(2,1)S(1)}, u32[]{:S(2)}) copy-start(bf16[2,320,128]{2,1,0:T(8,128)(2,1)S(1)} %collective-permute-done.8.refs_4_.refs_1_) | copy-start | bytes 491524
  41.6 4.2 %copy-start.14 = (bf16[2,320,128]{2,1,0:T(8,128)(2,1)}, bf16[2,320,128]{2,1,0:T(8,128)(2,1)S(1)}, u32[]{:S(2)}) copy-start(bf16[2,320,128]{2,1,0:T(8,128)(2,1)S(1)} %collective-permute-done.9.refs_5_.refs_2_) | copy-start | bytes 491524
  42.7 17.9 %copy-start.2 = (bf16[1280,128]{1,0:T(8,128)(2,1)}, bf16[1280,128]{1,0:T(8,128)(2,1)S(1)}, u32[]{:S(2)}) copy-start(bf16[1280,128]{1,0:T(8,128)(2,1)S(1)} %get-tuple-element.83.refs_3_.refs_0_) | copy-start | bytes 983044
  42.7 12.6 %collective-permute-start.11 = (bf16[1280,128]{1,0:T(8,128)(2,1)S(1)}, bf16[1280,128]{1,0:T(8,128)(2,1)S(1)}, u32[]{:S(2)}, u32[]{:S(2)}) collective-permute-start(bf16[1280,128]{1,0:T(8,128)(2,1)S(1)} %get-tuple-element.83.refs_3_.refs_0_), channel_id=1, source_target_pairs={{4,0},{8,4},{12,8},{0,12},{20,16},{24,20},{28,24},{16,28},{36,32},... | collective-permute-start | bytes 983048 | tf_op jit(solution)/shard_map/ppermute | solution.py:43
  44.1 12.2 %collective-permute-start.12 = (bf16[1280,128]{1,0:T(8,128)(2,1)S(1)}, bf16[1280,128]{1,0:T(8,128)(2,1)S(1)}, u32[]{:S(2)}, u32[]{:S(2)}) collective-permute-start(bf16[1280,128]{1,0:T(8,128)(2,1)S(1)} %get-tuple-element.83.refs_3_.refs_0_), channel_id=1, source_target_pairs={{8,0},{12,4},{0,8},{4,12},{24,16},{28,20},{16,24},{20,28},{40,32},... | collective-permute-start | bytes 983048 | tf_op jit(solution)/shard_map/ppermute | solution.py:43
  45.5 15.1 %collective-permute-start.13 = (bf16[1280,128]{1,0:T(8,128)(2,1)S(1)}, bf16[1280,128]{1,0:T(8,128)(2,1)S(1)}, u32[]{:S(2)}, u32[]{:S(2)}) collective-permute-start(bf16[1280,128]{1,0:T(8,128)(2,1)S(1)} %get-tuple-element.83.refs_3_.refs_0_), channel_id=1, source_target_pairs={{12,0},{0,4},{4,8},{8,12},{28,16},{16,20},{20,24},{24,28},{44,32},... | collective-permute-start | bytes 983048 | tf_op jit(solution)/shard_map/ppermute | solution.py:43
  45.8 1.6 copy-start.1
  51.4 0.9 copy-start.11
  52.3 0.9 copy-start.13
  53.2 0.9 copy-start.15
  55.3 5.3 %copy-start.4 = (bf16[1280,128]{1,0:T(8,128)(2,1)}, bf16[1280,128]{1,0:T(8,128)(2,1)S(1)}, u32[]{:S(2)}) copy-start(bf16[1280,128]{1,0:T(8,128)(2,1)S(1)} %collective-permute-done.11.refs_4_.refs_1_) | copy-start | bytes 983044
  56.3 4.3 %copy-start.6 = (bf16[1280,128]{1,0:T(8,128)(2,1)}, bf16[1280,128]{1,0:T(8,128)(2,1)S(1)}, u32[]{:S(2)}) copy-start(bf16[1280,128]{1,0:T(8,128)(2,1)S(1)} %collective-permute-done.12.refs_5_.refs_2_) | copy-start | bytes 983044
  60.6 0.7 copy-start.8
  60.6 7.5 %copy-start.18 = (bf16[1,1280]{1,0:T(2,128)(2,1)S(1)}, bf16[1,1280]{1,0:T(2,128)(2,1)}, u32[]{:S(2)}) copy-start(bf16[1,1280]{1,0:T(2,128)(2,1)} %gain.1) | copy-start | bytes 7684
  61.3 6.8 %collective-permute-start.14 = (bf16[1024,1280]{1,0:T(8,128)(2,1)S(1)}, bf16[1024,1280]{1,0:T(8,128)(2,1)}, u32[]{:S(2)}, u32[]{:S(2)}) collective-permute-start(bf16[1024,1280]{1,0:T(8,128)(2,1)S(1)} %shard_map.109.crossed), channel_id=1, source_target_pairs={{128,192},{129,193},{130,194},{131,195},{132,196},{133,197},{134,1... | collective-permute-start | bytes 7864328 | tf_op jit(solution)/shard_map/ppermute | solution.py:541
  63.4 14.6 %slice-start = ((s8[5242880]{0:T(1024)(128)(4,1)}), s8[4194304]{0:T(1024)(128)(4,1)S(1)}, s32[]{:S(2)}) async-start(s8[5242880]{0:T(1024)(128)(4,1)} %bitcast.19), calls=%async_computation.2 | async-start | bytes 8388608
  63.5 9.1 %copy-start.3 = (bf16[1280,128]{1,0:T(8,128)(2,1)S(1)}, bf16[1280,128]{1,0:T(8,128)(2,1)}, u32[]{:S(2)}) copy-start(bf16[1280,128]{1,0:T(8,128)(2,1)} %copy-done.2) | copy-start | bytes 983044
  63.5 9.1 %copy-start.5 = (bf16[1280,128]{1,0:T(8,128)(2,1)S(1)}, bf16[1280,128]{1,0:T(8,128)(2,1)}, u32[]{:S(2)}) copy-start(bf16[1280,128]{1,0:T(8,128)(2,1)} %copy-done.4) | copy-start | bytes 983044
  63.5 9.1 %copy-start.7 = (bf16[1280,128]{1,0:T(8,128)(2,1)S(1)}, bf16[1280,128]{1,0:T(8,128)(2,1)}, u32[]{:S(2)}) copy-start(bf16[1280,128]{1,0:T(8,128)(2,1)} %copy-done.6) | copy-start | bytes 983044
  63.5 9.1 %copy-start.9 = (bf16[1280,128]{1,0:T(8,128)(2,1)S(1)}, bf16[1280,128]{1,0:T(8,128)(2,1)}, u32[]{:S(2)}) copy-start(bf16[1280,128]{1,0:T(8,128)(2,1)} %copy-done.8) | copy-start | bytes 983044
  63.5 14.5 %slice-start.1 = ((s8[5242880]{0:T(1024)(128)(4,1)}), s8[1048576]{0:T(1024)(128)(4,1)S(1)}, s32[]{:S(2)}) async-start(s8[5242880]{0:T(1024)(128)(4,1)} %bitcast.19), calls=%async_computation.3 | async-start | bytes 2097152
  63.5 31.8 %collective-permute-start.15 = (bf16[2,1280,128]{2,1,0:T(8,128)(2,1)S(1)}, bf16[2,1280,128]{2,1,0:T(8,128)(2,1)S(1)}, u32[]{:S(2)}, u32[]{:S(2)}) collective-permute-start(bf16[2,1280,128]{2,1,0:T(8,128)(2,1)S(1)} %get-tuple-element.82.refs_2_.refs_0_), channel_id=1, source_target_pairs={{16,0},{20,4},{24,8},{28,12},{32,16},{36,20},{40,24},{44,28},{48,3... | collective-permute-start | bytes 1966088 | tf_op jit(solution)/shard_map/ppermute | solution.py:38
  67.2 28.2 %collective-permute-start.16 = (bf16[2,1280,128]{2,1,0:T(8,128)(2,1)S(1)}, bf16[2,1280,128]{2,1,0:T(8,128)(2,1)S(1)}, u32[]{:S(2)}, u32[]{:S(2)}) collective-permute-start(bf16[2,1280,128]{2,1,0:T(8,128)(2,1)S(1)} %get-tuple-element.82.refs_2_.refs_0_), channel_id=1, source_target_pairs={{32,0},{36,4},{40,8},{44,12},{48,16},{52,20},{56,24},{60,28},{0,32... | collective-permute-start | bytes 1966088 | tf_op jit(solution)/shard_map/ppermute | solution.py:38
  67.2 31.6 %collective-permute-start.17 = (bf16[2,1280,128]{2,1,0:T(8,128)(2,1)S(1)}, bf16[2,1280,128]{2,1,0:T(8,128)(2,1)S(1)}, u32[]{:S(2)}, u32[]{:S(2)}) collective-permute-start(bf16[2,1280,128]{2,1,0:T(8,128)(2,1)S(1)} %get-tuple-element.82.refs_2_.refs_0_), channel_id=1, source_target_pairs={{48,0},{52,4},{56,8},{60,12},{0,16},{4,20},{8,24},{12,28},{16,32},... | collective-permute-start | bytes 1966088 | tf_op jit(solution)/shard_map/ppermute | solution.py:38
  75.0 25.1 %collective-permute-start.18 = (bf16[528,512]{1,0:T(8,128)(2,1)S(1)}, bf16[528,512]{1,0:T(8,128)(2,1)S(1)}, u32[]{:S(2)}, u32[]{:S(2)}) collective-permute-start(bf16[528,512]{1,0:T(8,128)(2,1)S(1)} %get-tuple-element.89), channel_id=1, source_target_pairs={{0,1},{1,2},{2,3},{3,0},{4,5},{5,6},{6,7},{7,4},{8,9},{9,10},{10,1... | collective-permute-start | bytes 1622024 | tf_op jit(solution)/shard_map/ppermute | solution.py:33
  78.0 22.1 %collective-permute-start.19 = (bf16[512,512]{1,0:T(8,128)(2,1)S(1)}, bf16[512,512]{1,0:T(8,128)(2,1)S(1)}, u32[]{:S(2)}, u32[]{:S(2)}) collective-permute-start(bf16[512,512]{1,0:T(8,128)(2,1)S(1)} %get-tuple-element.90), channel_id=1, source_target_pairs={{0,3},{1,0},{2,1},{3,2},{4,7},{5,4},{6,5},{7,6},{8,11},{9,8},{10,9... | collective-permute-start | bytes 1572872 | tf_op jit(solution)/shard_map/ppermute | solution.py:33
  100.1 29.2 %copy-start.24 = (s32[4]{0:T(128)S(1)}, s32[4]{0:T(128)}, u32[]{:S(2)}) copy-start(s32[4]{0:T(128)} %param.14) | copy-start | bytes 52
  100.1 29.4 %copy-start.23 = (bf16[16,1024]{1,0:T(8,128)(2,1)S(1)}, bf16[16,1024]{1,0:T(8,128)(2,1)}, u32[]{:S(2)}) copy-start(bf16[16,1024]{1,0:T(8,128)(2,1)} %reshape_squeeze.6.queries) | copy-start | bytes 98308
  103.5 18.1 %collective-permute-start.20 = (bf16[1040,256]{1,0:T(8,128)(2,1)S(1)}, bf16[1040,256]{1,0:T(8,128)(2,1)S(1)}, u32[]{:S(2)}, u32[]{:S(2)}) collective-permute-start(bf16[1040,256]{1,0:T(8,128)(2,1)S(1)} %get-tuple-element.91), channel_id=1, source_target_pairs={{0,1},{1,2},{2,3},{3,0},{4,5},{5,6},{6,7},{7,4},{8,9},{9,10},{10,1... | collective-permute-start | bytes 1597448 | tf_op jit(solution)/shard_map/ppermute | solution.py:33
  104.7 20.5 %collective-permute-start.21 = (bf16[1040,256]{1,0:T(8,128)(2,1)S(1)}, bf16[1040,256]{1,0:T(8,128)(2,1)S(1)}, u32[]{:S(2)}, u32[]{:S(2)}) collective-permute-start(bf16[1040,256]{1,0:T(8,128)(2,1)S(1)} %get-tuple-element.92), channel_id=1, source_target_pairs={{0,3},{1,0},{2,1},{3,2},{4,7},{5,4},{6,5},{7,6},{8,11},{9,8},{10,9... | collective-permute-start | bytes 1597448 | tf_op jit(solution)/shard_map/ppermute | solution.py:33
  121.6 4.7 %copy-start.21 = (bf16[1040,256]{1,0:T(8,128)(2,1)}, bf16[1040,256]{1,0:T(8,128)(2,1)S(1)}, u32[]{:S(2)}) copy-start(bf16[1040,256]{1,0:T(8,128)(2,1)S(1)} %collective-permute-done.20.refs_0_) | copy-start | bytes 1597444
  125.2 4.1 %copy-start.22 = (bf16[1040,256]{1,0:T(8,128)(2,1)}, bf16[1040,256]{1,0:T(8,128)(2,1)S(1)}, u32[]{:S(2)}) copy-start(bf16[1040,256]{1,0:T(8,128)(2,1)S(1)} %collective-permute-done.21.refs_1_) | copy-start | bytes 1597444
  125.2 1.2 collective-permute-start.22
  126.3 34.6 %collective-permute-start.23 = (bf16[1024,256]{1,0:T(8,128)(2,1)S(1)}, bf16[1024,256]{1,0:T(8,128)(2,1)S(1)}, u32[]{:S(2)}, u32[]{:S(2)}) collective-permute-start(bf16[1024,256]{1,0:T(8,128)(2,1)S(1)} %get-tuple-element.99), channel_id=1, source_target_pairs={{0,1},{1,2},{2,3},{3,0},{4,5},{5,6},{6,7},{7,4},{8,9},{9,10},{10,1... | collective-permute-start | bytes 1572872 | tf_op jit(solution)/shard_map/ppermute | solution.py:33
  126.9 34.0 %collective-permute-start.24 = (bf16[1024,256]{1,0:T(8,128)(2,1)S(1)}, bf16[1024,256]{1,0:T(8,128)(2,1)S(1)}, u32[]{:S(2)}, u32[]{:S(2)}) collective-permute-start(bf16[1024,256]{1,0:T(8,128)(2,1)S(1)} %get-tuple-element.100), channel_id=1, source_target_pairs={{0,3},{1,0},{2,1},{3,2},{4,7},{5,4},{6,5},{7,6},{8,11},{9,8},{10,9... | collective-permute-start | bytes 1572872 | tf_op jit(solution)/shard_map/ppermute | solution.py:33
  160.9 1.0 copy-start.19
  163.7 26.2 %copy-start.20 = (bf16[16,8,16,256]{3,2,1,0:T(8,128)(2,1)S(1)}, bf16[16,8,16,256]{3,2,1,0:T(8,128)(2,1)}, u32[]{:S(2)}) copy-start(bf16[16,8,16,256]{3,2,1,0:T(8,128)(2,1)} %copy-done.19) | copy-start | bytes 3145732
